TPU v7x, 32 devices: a whole 2x2x4 slice. The times are simulated.
32 devices in a mesh: sys: 2 (over y), row: 4 (over z), col: 4 (over x, core).
Axes of the slice: x: 2, y: 2, z: 4, core: 2. Of those that a mesh axis runs over, the one named last changes fastest.
Arguments:
- a_blocks: bfloat16 [8, 64, 4096], P(('sys', 'row'), 'col'), parts along dimension 0, may hold values from -0.75 to 0.75
- a_index: int32 [2, 8, 64], P(None, ('sys', 'row'), 'col'), parts along dimension 1, may hold values from -1 to 15, as said below
- b_blocks: bfloat16 [128, 16, 4096], P(('sys', 'row'), 'col'), parts along dimension 0, may hold values from -4 to 4
- b_cols: int32 [128, 16], P(('sys', 'row'), 'col'), parts along dimension 0, may hold values from -1 to 15, as said below
- c_cols: int32 [128, 16], P(('sys', 'row'), 'col'), parts along dimension 0, may hold values from 0 to 15, as said below
Outputs:
- c_blocks: float32 [128, 16, 4096], P(('sys', 'row'), 'col'), parts along dimension 0
There are 2 independent parts, one for each index of `sys`. A program takes and returns all parts, laid end to end along the dimension named above; each array names one. Nothing has to cross between parts.
Inputs may be any that keep to these rules, and one draw needn't show every extreme that they name: a_index[0] is -1 for an empty slot; the live slots of one entry (p, g) name distinct blocks; some entry has all 16 slots live and some entry only one. `b_cols`: -1 marks an empty slot; the live entries of one block row within one column group are distinct; some block row has all 4 slots of a column group live and some only one. `c_cols`: the 4 entries of one block row within one column group are distinct.
All inputs are finite; a program needn't handle non-finite values.
Results may differ from a plain program's by a relative error of at most 0.0003.
Values may be sent and summed in bfloat16 or wider, within the bound.
No kernel may reach another device: no remote copies, remote signals or barrier semaphores. Data moves between devices by JAX's collectives and lax.ppermute only.
A program may use at most 64 MiB of HBM per device.

v0:
```python
import jax
import jax.numpy as jnp
from jax import lax
from jax.sharding import PartitionSpec as P

BS = 64


def from_behind(block, axis, distance):
    devices = range(lax.axis_size(axis))
    route = [((i - distance) % len(devices), i) for i in devices]
    return lax.ppermute(block, axis, route)


def for_sending(value):

    def short(part):
        return part.astype(jnp.bfloat16) if part.dtype == jnp.float32 else part

    return jax.tree.map(short, value)


def contribute(a_values, a_rows, a_inner, b_values, b_columns, c_columns):
    slot_total = a_values.shape[0]
    row_count = b_values.shape[0]
    offer_count = b_values.shape[1]
    kept_count = c_columns.shape[1]
    safe_rows = jnp.maximum(a_rows, 0)
    wanted = c_columns[safe_rows]
    offered = b_columns[a_inner]
    matches = wanted[:, :, None] == offered[:, None, :]
    located = jnp.any(matches, axis=2)
    position = jnp.sum(jnp.where(matches, jnp.arange(offer_count, dtype=jnp.int32), 0), axis=2)
    picked = b_values.reshape(row_count * offer_count, BS * BS)[
        a_inner[:, None] * offer_count + position
    ]
    picked = jnp.where(located[:, :, None], picked, jnp.zeros((), picked.dtype))
    left_blocks = a_values.reshape(slot_total, BS, BS)
    products = jnp.einsum(
        "sxj,smjk->sxmk",
        left_blocks,
        picked.reshape(slot_total, kept_count, BS, BS),
        preferred_element_type=jnp.float32,
    )
    owners = (a_rows[None, :] == jnp.arange(row_count, dtype=jnp.int32)[:, None]).astype(
        jnp.float32
    )
    return jnp.einsum("rs,sxmk->rxmk", owners, products, precision=lax.Precision.HIGHEST)


def expand_like(mask, target):
    return mask.reshape(mask.shape + (1,) * (target.ndim - 1))


def shards(a_blocks, a_index, b_blocks, b_cols, c_cols):
    row_count = lax.axis_size("row")
    col_count = lax.axis_size("col")
    per_col = row_count // col_count
    grid_row = lax.axis_index("row")
    grid_col = lax.axis_index("col")
    slot_total = a_blocks.shape[1] // per_col
    a_values = a_blocks.reshape(per_col, slot_total, a_blocks.shape[2])
    a_rows = a_index[0, 0].reshape(per_col, slot_total)
    a_inner = a_index[1, 0].reshape(per_col, slot_total)
    totals = jnp.zeros((b_blocks.shape[0], BS, c_cols.shape[1], BS), jnp.float32)
    bit_total = (col_count - 1).bit_length()
    b_current = b_blocks
    b_current_cols = b_cols
    for bit_number in range(bit_total):
        arrived = from_behind((b_current, b_current_cols), "row", -(per_col << bit_number))
        taking = grid_col >> bit_number & 1 == 1
        b_current = jnp.where(taking, arrived[0], b_current)
        b_current_cols = jnp.where(taking, arrived[1], b_current_cols)
    offsets = jnp.arange(per_col, dtype=jnp.int32)
    source = (grid_row - offsets) % per_col
    distance = (grid_row - offsets) // per_col % col_count
    holding = tuple((own_part[source] for own_part in (a_values, a_rows, a_inner)))
    for bit_number in range(bit_total):
        arrived = jax.tree.map(
            lambda part, own: part.astype(own.dtype),
            from_behind(for_sending(holding), "col", -(1 << bit_number)),
            holding,
        )
        taking = distance >> bit_number & 1 == 1
        holding = tuple(
            (
                jnp.where(expand_like(taking, old_part), new_part, old_part)
                for new_part, old_part in zip(arrived, holding)
            )
        )

    def advance(step_index, state_tuple):
        running, b_now, b_now_cols, waiting_values, waiting_rows, waiting_inner = state_tuple
        place = step_index % per_col
        using_values = lax.dynamic_index_in_dim(waiting_values, place, 0, keepdims=False)
        using_rows = lax.dynamic_index_in_dim(waiting_rows, place, 0, keepdims=False)
        using_inner = lax.dynamic_index_in_dim(waiting_inner, place, 0, keepdims=False)
        running = running + contribute(
            using_values, using_rows, using_inner, b_now, b_now_cols, c_cols
        )
        b_now, b_now_cols = (
            from_behind(b_now, "row", 1),
            from_behind(for_sending(b_now_cols), "row", 1).astype(b_now_cols.dtype),
        )
        passed = (
            from_behind(using_values, "col", 1),
            from_behind(for_sending(using_rows), "col", 1).astype(using_rows.dtype),
            from_behind(for_sending(using_inner), "col", 1).astype(using_inner.dtype),
        )
        waiting_values = lax.dynamic_update_index_in_dim(waiting_values, passed[0], place, 0)
        waiting_rows = lax.dynamic_update_index_in_dim(waiting_rows, passed[1], place, 0)
        waiting_inner = lax.dynamic_update_index_in_dim(waiting_inner, passed[2], place, 0)
        return (running, b_now, b_now_cols, waiting_values, waiting_rows, waiting_inner)

    finished = lax.fori_loop(
        0, row_count - 1, advance, (totals, b_current, b_current_cols) + holding
    )
    final_place = (row_count - 1) % per_col
    totals = finished[0] + contribute(
        finished[3][final_place],
        finished[4][final_place],
        finished[5][final_place],
        finished[1],
        finished[2],
        c_cols,
    )
    ordered = jnp.transpose(totals, (0, 2, 1, 3))
    return ordered.reshape(ordered.shape[0], ordered.shape[1], BS * BS)


def solution(mesh):
    return jax.shard_map(
        shards,
        mesh=mesh,
        in_specs=(
            P(("sys", "row"), "col", None),
            P(None, ("sys", "row"), "col"),
            P(("sys", "row"), "col", None),
            P(("sys", "row"), "col"),
            P(("sys", "row"), "col"),
        ),
        out_specs=P(("sys", "row"), "col", None),
        check_vma=False,
    )
```

profile of v0, /device:TPU:0, one launch (start us, length us, event | category | flops | bytes accessed | tf_op | source)
XLA Modules:
  0.0 135.1 jit_solution(3564052329131714933)
XLA Ops:
  0.0 2.4 %collective-permute-start.9 = (bf16[1,16,4096]{2,1,0:T(8,128)(2,1)}, bf16[1,16,4096]{2,1,0:T(8,128)(2,1)S(1)}, u32[]{:S(2)}, u32[]{:S(2)}) collective-permute-start(bf16[1,16,4096]{2,1,0:T(8,128)(2,1)} %param.7), channel_id=1, source_target_pairs={{1,0},{2,1},{3,2},{0,3},{5,4},{6,5},{7,6},{4,7},{9,8},{10,9},{11,1... | collective-permute-start | bytes 393224 | tf_op jit(solution)/shard_map/ppermute | solution.py:12
  4.5 3.6 %collective-permute-start.7 = (s32[16,4]{1,0:T(8,128)S(1)}, s32[16,4]{1,0:T(8,128)S(1)}, u32[]{:S(2)}, u32[]{:S(2)}) collective-permute-start(s32[16,4]{1,0:T(8,128)S(1)} %copy.26), channel_id=1, source_target_pairs={{4,0},{8,4},{12,8},{0,12},{5,1},{9,5},{13,9},{1,13},{6,2},{10,6},{... | collective-permute-start | bytes 776 | tf_op jit(solution)/shard_map/ppermute | solution.py:12
  10.0 1.4 %collective-permute-start.14 = (s32[1,16]{1,0:T(1,128)S(1)}, s32[1,16]{1,0:T(1,128)S(1)}, u32[]{:S(2)}, u32[]{:S(2)}) collective-permute-start(s32[1,16]{1,0:T(1,128)S(1)} %get-tuple-element.213), channel_id=1, source_target_pairs={{2,0},{3,1},{0,2},{1,3},{6,4},{7,5},{4,6},{5,7},{10,8},{11,9},{8,1... | collective-permute-start | bytes 200 | tf_op jit(solution)/shard_map/ppermute | solution.py:12
  12.0 1.5 %collective-permute-done.14 = s32[1,16]{1,0:T(1,128)S(1)} collective-permute-done((s32[1,16]{1,0:T(1,128)S(1)}, s32[1,16]{1,0:T(1,128)S(1)}, u32[]{:S(2)}, u32[]{:S(2)}) %collective-permute-start.14) | collective-permute-done | bytes 96 | tf_op jit(solution)/shard_map/ppermute | solution.py:12
  15.5 5.8 %collective-permute-done.8 = s32[16,4]{1,0:T(8,128)S(1)} collective-permute-done((s32[16,4]{1,0:T(8,128)S(1)}, s32[16,4]{1,0:T(8,128)S(1)}, u32[]{:S(2)}, u32[]{:S(2)}) %collective-permute-start.8) | collective-permute-done | bytes 288 | tf_op jit(solution)/shard_map/ppermute | solution.py:12
  24.6 3.5 %collective-permute-start.6 = (bf16[16,4,4096]{2,1,0:T(4,128)(2,1)S(1)}, bf16[16,4,4096]{2,1,0:T(4,128)(2,1)S(1)}, u32[]{:S(2)}, u32[]{:S(2)}) collective-permute-start(bf16[16,4,4096]{2,1,0:T(4,128)(2,1)S(1)} %bitcast.106), channel_id=1, source_target_pairs={{8,0},{12,4},{0,8},{4,12},{9,1},{13,5},{1,9},{5,13},{10,2},{14,6},... | collective-permute-start | bytes 1572872 | tf_op jit(solution)/shard_map/ppermute | solution.py:12
  28.8 19.4 %collective-permute-done.6 = bf16[16,4,4096]{2,1,0:T(4,128)(2,1)S(1)} collective-permute-done((bf16[16,4,4096]{2,1,0:T(4,128)(2,1)S(1)}, bf16[16,4,4096]{2,1,0:T(4,128)(2,1)S(1)}, u32[]{:S(2)}, u32[]{:S(2)}) %collective-permute-start.6) | collective-permute-done | bytes 524320 | tf_op jit(solution)/shard_map/ppermute | solution.py:12
  48.3 72.1 %while.24 = (s32[]{:T(128)}, f32[16,64,4,64]{3,0,2,1:T(8,128)}, bf16[16,4,4096]{2,1,0:T(4,128)(2,1)S(1)}, s32[16,4]{1,0:T(8,128)}, bf16[1,16,4096]{2,1,0:T(8,128...) while((s32[]{:T(128)}, f32[16,64,4,64]{3,0,2,1:T(8,128)}, ...), condition=%wide.region_3.4_spmd.clone, body=%wide.region_0.3_spmd.clone.sunk | while | flops 84677328 | bytes 15356727 | solution.py:115
  48.3 1.2 copy.69
  49.5 1.2 copy.70
  50.7 1.6 %collective-permute-start.4 = (s32[16]{0:T(128)}, s32[16]{0:T(128)}, u32[]{:S(2)}, u32[]{:S(2)}) collective-permute-start(s32[16]{0:T(128)} %bitcast.102), channel_id=1, source_target_pairs={{3,0},{0,1},{1,2},{2,3},{7,4},{4,5},{5,6},{6,7},{11,8},{8,9},{9,10... | collective-permute-start | bytes 200 | tf_op jit(solution)/shard_map/while/body/eval_jaxpr/ppermute | solution.py:12
  59.5 1.1 gather.70
  62.1 1.8 %convolution_bitcast_fusion.2 = f32[16,64,4,64]{1,3,2,0:T(8,128)} fusion(bf16[16,4,64,64]{2,3,1,0:T(8,128)(2,1)S(1)} %copy.54, pred[16,4]{1,0:T(8,128)(4,1)S(1)} %copy.55, bf16[16,64,64,1]{2,1,0,3:T(8,128)(2,1)S(1)} %reshape.333), kind=kOutput, calls=%fused_computation.7.clone.1 | convolution fusion | flops 33816576 | bytes 1704000 | tf_op jit(solution)/shard_map/while/body/eval_jaxpr/sxj,smjk->sxmk/dot_general | solution.py:39
  63.9 3.1 %copy.56 = f32[16,64,4,64]{3,0,2,1:T(8,128)S(1)} copy(f32[16,64,4,64]{1,3,2,0:T(8,128)} %convolution_bitcast_fusion.2) | data formatting | bytes 2097152 | tf_op jit(solution)/shard_map/while/body/eval_jaxpr/sxj,smjk->sxmk/dot_general | solution.py:39
  67.0 3.2 %select_add_fusion.2 = f32[16,64,4,64]{3,0,2,1:T(8,128)} fusion(f32[16,64,4,64]{3,0,2,1:T(8,128)} %get-tuple-element.279, f32[16,64,4,64]{3,0,2,1:T(8,128)S(1)} %copy.56, pred[]{:T(512)S(6)} %compare.6, s32[16]{0:T(128)} %bitcast.98), kind=kOutput, calls=%fused_computation.6.clone.1 | convolution fusion | flops 50856192 | bytes 3145793 | tf_op jit(solution)/shard_map/while/body/eval_jaxpr/rs,sxmk->rxmk/dot_general | solution.py:48
  70.2 1.2 copy.69
  71.9 1.2 copy.70
  73.4 3.7 %collective-permute-start = (bf16[16,4,4096]{2,1,0:T(4,128)(2,1)S(1)}, bf16[16,4,4096]{2,1,0:T(4,128)(2,1)S(1)}, u32[]{:S(2)}, u32[]{:S(2)}) collective-permute-start(bf16[16,4,4096]{2,1,0:T(4,128)(2,1)S(1)} %copy.66), channel_id=1, source_target_pairs={{12,0},{0,4},{4,8},{8,12},{13,1},{1,5},{5,9},{9,13},{14,2},{2,6},{... | collective-permute-start | bytes 1572872 | tf_op jit(solution)/shard_map/while/body/eval_jaxpr/ppermute | solution.py:12
  78.7 2.3 %collective-permute-start.1 = (s32[16,4]{1,0:T(8,128)S(1)}, s32[16,4]{1,0:T(8,128)}, u32[]{:S(2)}, u32[]{:S(2)}) collective-permute-start(s32[16,4]{1,0:T(8,128)S(1)} %copy.67), channel_id=1, source_target_pairs={{12,0},{0,4},{4,8},{8,12},{13,1},{1,5},{5,9},{9,13},{14,2},{2,6},{... | collective-permute-start | bytes 776 | tf_op jit(solution)/shard_map/while/body/eval_jaxpr/ppermute | solution.py:12
  88.8 1.8 %convolution_bitcast_fusion.2 = f32[16,64,4,64]{1,3,2,0:T(8,128)} fusion(bf16[16,4,64,64]{2,3,1,0:T(8,128)(2,1)S(1)} %copy.54, pred[16,4]{1,0:T(8,128)(4,1)S(1)} %copy.55, bf16[16,64,64,1]{2,1,0,3:T(8,128)(2,1)S(1)} %reshape.333), kind=kOutput, calls=%fused_computation.7.clone.1 | convolution fusion | flops 33816576 | bytes 1704000 | tf_op jit(solution)/shard_map/while/body/eval_jaxpr/sxj,smjk->sxmk/dot_general | solution.py:39
  90.6 3.1 %copy.56 = f32[16,64,4,64]{3,0,2,1:T(8,128)S(1)} copy(f32[16,64,4,64]{1,3,2,0:T(8,128)} %convolution_bitcast_fusion.2) | data formatting | bytes 2097152 | tf_op jit(solution)/shard_map/while/body/eval_jaxpr/sxj,smjk->sxmk/dot_general | solution.py:39
  93.7 4.1 %select_add_fusion.2 = f32[16,64,4,64]{3,0,2,1:T(8,128)} fusion(f32[16,64,4,64]{3,0,2,1:T(8,128)} %get-tuple-element.279, f32[16,64,4,64]{3,0,2,1:T(8,128)S(1)} %copy.56, pred[]{:T(512)S(6)} %compare.6, s32[16]{0:T(128)} %bitcast.98), kind=kOutput, calls=%fused_computation.6.clone.1 | convolution fusion | flops 50856192 | bytes 3145793 | tf_op jit(solution)/shard_map/while/body/eval_jaxpr/rs,sxmk->rxmk/dot_general | solution.py:48
  97.9 1.2 copy.69
  99.4 1.2 copy.70
  111.1 1.8 %convolution_bitcast_fusion.2 = f32[16,64,4,64]{1,3,2,0:T(8,128)} fusion(bf16[16,4,64,64]{2,3,1,0:T(8,128)(2,1)S(1)} %copy.54, pred[16,4]{1,0:T(8,128)(4,1)S(1)} %copy.55, bf16[16,64,64,1]{2,1,0,3:T(8,128)(2,1)S(1)} %reshape.333), kind=kOutput, calls=%fused_computation.7.clone.1 | convolution fusion | flops 33816576 | bytes 1704000 | tf_op jit(solution)/shard_map/while/body/eval_jaxpr/sxj,smjk->sxmk/dot_general | solution.py:39
  112.9 3.1 %copy.56 = f32[16,64,4,64]{3,0,2,1:T(8,128)S(1)} copy(f32[16,64,4,64]{1,3,2,0:T(8,128)} %convolution_bitcast_fusion.2) | data formatting | bytes 2097152 | tf_op jit(solution)/shard_map/while/body/eval_jaxpr/sxj,smjk->sxmk/dot_general | solution.py:39
  116.0 4.1 %select_add_fusion.2 = f32[16,64,4,64]{3,0,2,1:T(8,128)} fusion(f32[16,64,4,64]{3,0,2,1:T(8,128)} %get-tuple-element.279, f32[16,64,4,64]{3,0,2,1:T(8,128)S(1)} %copy.56, pred[]{:T(512)S(6)} %compare.6, s32[16]{0:T(128)} %bitcast.98), kind=kOutput, calls=%fused_computation.6.clone.1 | convolution fusion | flops 50856192 | bytes 3145793 | tf_op jit(solution)/shard_map/while/body/eval_jaxpr/rs,sxmk->rxmk/dot_general | solution.py:48
  122.4 1.3 gather_fusion.4
  126.2 1.2 reshape.311
  127.9 3.5 %fusion.10 = f32[16,64,4,64]{3,0,2,1:T(8,128)S(1)} fusion(f32[16,64,4,64]{3,1,2,0:T(8,128)S(1)} %fusion.12, s32[16]{0:T(128)} %bitcast.5), kind=kOutput, calls=%fused_computation.28 | convolution fusion | flops 50331904 | bytes 2097216 | tf_op jit(solution)/shard_map/rs,sxmk->rxmk/dot_general | solution.py:48
  132.0 1.2 copy.41
  133.2 1.8 %reshape.314 = f32[16,4,4096]{2,1,0:T(4,128)} reshape(f32[16,4,64,64]{3,2,1,0:T(8,128)S(1)} %copy.41) | data formatting | bytes 2097152 | tf_op jit(solution)/shard_map/reshape | solution.py:128
  (145 shorter events, 45.7 us)
Async XLA Ops:
  0.0 21.9 %collective-permute-start.9 = (bf16[1,16,4096]{2,1,0:T(8,128)(2,1)}, bf16[1,16,4096]{2,1,0:T(8,128)(2,1)S(1)}, u32[]{:S(2)}, u32[]{:S(2)}) collective-permute-start(bf16[1,16,4096]{2,1,0:T(8,128)(2,1)} %param.7), channel_id=1, source_target_pairs={{1,0},{2,1},{3,2},{0,3},{5,4},{6,5},{7,6},{4,7},{9,8},{10,9},{11,1... | collective-permute-start | bytes 393224 | tf_op jit(solution)/shard_map/ppermute | solution.py:12
  3.1 6.3 %collective-permute-start.11 = (s32[1,16]{1,0:T(1,128)S(1)}, s32[1,16]{1,0:T(1,128)S(1)}, u32[]{:S(2)}, u32[]{:S(2)}) collective-permute-start(s32[1,16]{1,0:T(1,128)S(1)} %get-tuple-element.216), channel_id=1, source_target_pairs={{1,0},{2,1},{3,2},{0,3},{5,4},{6,5},{7,6},{4,7},{9,8},{10,9},{11,1... | collective-permute-start | bytes 200 | tf_op jit(solution)/shard_map/ppermute | solution.py:12
  3.7 5.6 %collective-permute-start.13 = (s32[1,16]{1,0:T(1,128)S(1)}, s32[1,16]{1,0:T(1,128)S(1)}, u32[]{:S(2)}, u32[]{:S(2)}) collective-permute-start(s32[1,16]{1,0:T(1,128)S(1)} %get-tuple-element.215), channel_id=1, source_target_pairs={{1,0},{2,1},{3,2},{0,3},{5,4},{6,5},{7,6},{4,7},{9,8},{10,9},{11,1... | collective-permute-start | bytes 200 | tf_op jit(solution)/shard_map/ppermute | solution.py:12
  4.5 9.6 %collective-permute-start.7 = (s32[16,4]{1,0:T(8,128)S(1)}, s32[16,4]{1,0:T(8,128)S(1)}, u32[]{:S(2)}, u32[]{:S(2)}) collective-permute-start(s32[16,4]{1,0:T(8,128)S(1)} %copy.26), channel_id=1, source_target_pairs={{4,0},{8,4},{12,8},{0,12},{5,1},{9,5},{13,9},{1,13},{6,2},{10,6},{... | collective-permute-start | bytes 776 | tf_op jit(solution)/shard_map/ppermute | solution.py:12
  8.9 14.7 %collective-permute-start.5 = (bf16[16,4,4096]{2,1,0:T(4,128)(2,1)}, bf16[16,4,4096]{2,1,0:T(4,128)(2,1)S(1)}, u32[]{:S(2)}, u32[]{:S(2)}) collective-permute-start(bf16[16,4,4096]{2,1,0:T(4,128)(2,1)} %param.9), channel_id=1, source_target_pairs={{4,0},{8,4},{12,8},{0,12},{5,1},{9,5},{13,9},{1,13},{6,2},{10,6},{... | collective-permute-start | bytes 1572872 | tf_op jit(solution)/shard_map/ppermute | solution.py:12
  10.0 3.5 %collective-permute-start.14 = (s32[1,16]{1,0:T(1,128)S(1)}, s32[1,16]{1,0:T(1,128)S(1)}, u32[]{:S(2)}, u32[]{:S(2)}) collective-permute-start(s32[1,16]{1,0:T(1,128)S(1)} %get-tuple-element.213), channel_id=1, source_target_pairs={{2,0},{3,1},{0,2},{1,3},{6,4},{7,5},{4,6},{5,7},{10,8},{11,9},{8,1... | collective-permute-start | bytes 200 | tf_op jit(solution)/shard_map/ppermute | solution.py:12
  11.4 3.5 %collective-permute-start.12 = (s32[1,16]{1,0:T(1,128)S(1)}, s32[1,16]{1,0:T(1,128)S(1)}, u32[]{:S(2)}, u32[]{:S(2)}) collective-permute-start(s32[1,16]{1,0:T(1,128)S(1)} %get-tuple-element.214), channel_id=1, source_target_pairs={{2,0},{3,1},{0,2},{1,3},{6,4},{7,5},{4,6},{5,7},{10,8},{11,9},{8,1... | collective-permute-start | bytes 200 | tf_op jit(solution)/shard_map/ppermute | solution.py:12
  14.1 7.2 %collective-permute-start.8 = (s32[16,4]{1,0:T(8,128)S(1)}, s32[16,4]{1,0:T(8,128)S(1)}, u32[]{:S(2)}, u32[]{:S(2)}) collective-permute-start(s32[16,4]{1,0:T(8,128)S(1)} %broadcast_select_fusion.4), channel_id=1, source_target_pairs={{8,0},{12,4},{0,8},{4,12},{9,1},{13,5},{1,9},{5,13},{10,2},{14,6},... | collective-permute-start | bytes 776 | tf_op jit(solution)/shard_map/ppermute | solution.py:12
  22.8 5.3 %collective-permute-start.10 = (bf16[1,16,4096]{2,1,0:T(8,128)(2,1)S(1)}, bf16[1,16,4096]{2,1,0:T(8,128)(2,1)S(1)}, u32[]{:S(2)}, u32[]{:S(2)}) collective-permute-start(bf16[1,16,4096]{2,1,0:T(8,128)(2,1)S(1)} %broadcast_select_fusion.2), channel_id=1, source_target_pairs={{2,0},{3,1},{0,2},{1,3},{6,4},{7,5},{4,6},{5,7},{10,8},{11,9},{8,1... | collective-permute-start | bytes 393224 | tf_op jit(solution)/shard_map/ppermute | solution.py:12
  24.6 23.6 %collective-permute-start.6 = (bf16[16,4,4096]{2,1,0:T(4,128)(2,1)S(1)}, bf16[16,4,4096]{2,1,0:T(4,128)(2,1)S(1)}, u32[]{:S(2)}, u32[]{:S(2)}) collective-permute-start(bf16[16,4,4096]{2,1,0:T(4,128)(2,1)S(1)} %bitcast.106), channel_id=1, source_target_pairs={{8,0},{12,4},{0,8},{4,12},{9,1},{13,5},{1,9},{5,13},{10,2},{14,6},... | collective-permute-start | bytes 1572872 | tf_op jit(solution)/shard_map/ppermute | solution.py:12
  49.5 20.7 %collective-permute-start.3 = (s32[16]{0:T(128)}, s32[16]{0:T(128)}, u32[]{:S(2)}, u32[]{:S(2)}) collective-permute-start(s32[16]{0:T(128)} %bitcast.98), channel_id=1, source_target_pairs={{3,0},{0,1},{1,2},{2,3},{7,4},{4,5},{5,6},{6,7},{11,8},{8,9},{9,10... | collective-permute-start | bytes 200 | tf_op jit(solution)/shard_map/while/body/eval_jaxpr/ppermute | solution.py:12
  50.7 19.5 %collective-permute-start.4 = (s32[16]{0:T(128)}, s32[16]{0:T(128)}, u32[]{:S(2)}, u32[]{:S(2)}) collective-permute-start(s32[16]{0:T(128)} %bitcast.102), channel_id=1, source_target_pairs={{3,0},{0,1},{1,2},{2,3},{7,4},{4,5},{5,6},{6,7},{11,8},{8,9},{9,10... | collective-permute-start | bytes 200 | tf_op jit(solution)/shard_map/while/body/eval_jaxpr/ppermute | solution.py:12
  52.5 17.7 %collective-permute-start = (bf16[16,4,4096]{2,1,0:T(4,128)(2,1)S(1)}, bf16[16,4,4096]{2,1,0:T(4,128)(2,1)S(1)}, u32[]{:S(2)}, u32[]{:S(2)}) collective-permute-start(bf16[16,4,4096]{2,1,0:T(4,128)(2,1)S(1)} %copy.66), channel_id=1, source_target_pairs={{12,0},{0,4},{4,8},{8,12},{13,1},{1,5},{5,9},{9,13},{14,2},{2,6},{... | collective-permute-start | bytes 1572872 | tf_op jit(solution)/shard_map/while/body/eval_jaxpr/ppermute | solution.py:12
  53.5 16.7 %collective-permute-start.2 = (bf16[16,4096]{1,0:T(8,128)(2,1)S(1)}, bf16[16,4096]{1,0:T(8,128)(2,1)}, u32[]{:S(2)}, u32[]{:S(2)}) collective-permute-start(bf16[16,4096]{1,0:T(8,128)(2,1)S(1)} %bitcast.105), channel_id=1, source_target_pairs={{3,0},{0,1},{1,2},{2,3},{7,4},{4,5},{5,6},{6,7},{11,8},{8,9},{9,10... | collective-permute-start | bytes 393224 | tf_op jit(solution)/shard_map/while/body/eval_jaxpr/ppermute | solution.py:12
  54.2 16.0 %collective-permute-start.1 = (s32[16,4]{1,0:T(8,128)S(1)}, s32[16,4]{1,0:T(8,128)}, u32[]{:S(2)}, u32[]{:S(2)}) collective-permute-start(s32[16,4]{1,0:T(8,128)S(1)} %copy.67), channel_id=1, source_target_pairs={{12,0},{0,4},{4,8},{8,12},{13,1},{1,5},{5,9},{9,13},{14,2},{2,6},{... | collective-permute-start | bytes 776 | tf_op jit(solution)/shard_map/while/body/eval_jaxpr/ppermute | solution.py:12
  71.4 26.4 %collective-permute-start.3 = (s32[16]{0:T(128)}, s32[16]{0:T(128)}, u32[]{:S(2)}, u32[]{:S(2)}) collective-permute-start(s32[16]{0:T(128)} %bitcast.98), channel_id=1, source_target_pairs={{3,0},{0,1},{1,2},{2,3},{7,4},{4,5},{5,6},{6,7},{11,8},{8,9},{9,10... | collective-permute-start | bytes 200 | tf_op jit(solution)/shard_map/while/body/eval_jaxpr/ppermute | solution.py:12
  73.1 24.8 %collective-permute-start.4 = (s32[16]{0:T(128)}, s32[16]{0:T(128)}, u32[]{:S(2)}, u32[]{:S(2)}) collective-permute-start(s32[16]{0:T(128)} %bitcast.102), channel_id=1, source_target_pairs={{3,0},{0,1},{1,2},{2,3},{7,4},{4,5},{5,6},{6,7},{11,8},{8,9},{9,10... | collective-permute-start | bytes 200 | tf_op jit(solution)/shard_map/while/body/eval_jaxpr/ppermute | solution.py:12
  73.4 24.5 %collective-permute-start = (bf16[16,4,4096]{2,1,0:T(4,128)(2,1)S(1)}, bf16[16,4,4096]{2,1,0:T(4,128)(2,1)S(1)}, u32[]{:S(2)}, u32[]{:S(2)}) collective-permute-start(bf16[16,4,4096]{2,1,0:T(4,128)(2,1)S(1)} %copy.66), channel_id=1, source_target_pairs={{12,0},{0,4},{4,8},{8,12},{13,1},{1,5},{5,9},{9,13},{14,2},{2,6},{... | collective-permute-start | bytes 1572872 | tf_op jit(solution)/shard_map/while/body/eval_jaxpr/ppermute | solution.py:12
  78.0 19.8 %collective-permute-start.2 = (bf16[16,4096]{1,0:T(8,128)(2,1)S(1)}, bf16[16,4096]{1,0:T(8,128)(2,1)}, u32[]{:S(2)}, u32[]{:S(2)}) collective-permute-start(bf16[16,4096]{1,0:T(8,128)(2,1)S(1)} %bitcast.105), channel_id=1, source_target_pairs={{3,0},{0,1},{1,2},{2,3},{7,4},{4,5},{5,6},{6,7},{11,8},{8,9},{9,10... | collective-permute-start | bytes 393224 | tf_op jit(solution)/shard_map/while/body/eval_jaxpr/ppermute | solution.py:12
  78.7 19.1 %collective-permute-start.1 = (s32[16,4]{1,0:T(8,128)S(1)}, s32[16,4]{1,0:T(8,128)}, u32[]{:S(2)}, u32[]{:S(2)}) collective-permute-start(s32[16,4]{1,0:T(8,128)S(1)} %copy.67), channel_id=1, source_target_pairs={{12,0},{0,4},{4,8},{8,12},{13,1},{1,5},{5,9},{9,13},{14,2},{2,6},{... | collective-permute-start | bytes 776 | tf_op jit(solution)/shard_map/while/body/eval_jaxpr/ppermute | solution.py:12
  99.1 21.1 %collective-permute-start.3 = (s32[16]{0:T(128)}, s32[16]{0:T(128)}, u32[]{:S(2)}, u32[]{:S(2)}) collective-permute-start(s32[16]{0:T(128)} %bitcast.98), channel_id=1, source_target_pairs={{3,0},{0,1},{1,2},{2,3},{7,4},{4,5},{5,6},{6,7},{11,8},{8,9},{9,10... | collective-permute-start | bytes 200 | tf_op jit(solution)/shard_map/while/body/eval_jaxpr/ppermute | solution.py:12
  100.6 19.6 %collective-permute-start.4 = (s32[16]{0:T(128)}, s32[16]{0:T(128)}, u32[]{:S(2)}, u32[]{:S(2)}) collective-permute-start(s32[16]{0:T(128)} %bitcast.102), channel_id=1, source_target_pairs={{3,0},{0,1},{1,2},{2,3},{7,4},{4,5},{5,6},{6,7},{11,8},{8,9},{9,10... | collective-permute-start | bytes 200 | tf_op jit(solution)/shard_map/while/body/eval_jaxpr/ppermute | solution.py:12
  101.1 19.1 %collective-permute-start = (bf16[16,4,4096]{2,1,0:T(4,128)(2,1)S(1)}, bf16[16,4,4096]{2,1,0:T(4,128)(2,1)S(1)}, u32[]{:S(2)}, u32[]{:S(2)}) collective-permute-start(bf16[16,4,4096]{2,1,0:T(4,128)(2,1)S(1)} %copy.66), channel_id=1, source_target_pairs={{12,0},{0,4},{4,8},{8,12},{13,1},{1,5},{5,9},{9,13},{14,2},{2,6},{... | collective-permute-start | bytes 1572872 | tf_op jit(solution)/shard_map/while/body/eval_jaxpr/ppermute | solution.py:12
  102.3 17.9 %collective-permute-start.2 = (bf16[16,4096]{1,0:T(8,128)(2,1)S(1)}, bf16[16,4096]{1,0:T(8,128)(2,1)}, u32[]{:S(2)}, u32[]{:S(2)}) collective-permute-start(bf16[16,4096]{1,0:T(8,128)(2,1)S(1)} %bitcast.105), channel_id=1, source_target_pairs={{3,0},{0,1},{1,2},{2,3},{7,4},{4,5},{5,6},{6,7},{11,8},{8,9},{9,10... | collective-permute-start | bytes 393224 | tf_op jit(solution)/shard_map/while/body/eval_jaxpr/ppermute | solution.py:12
  103.0 17.1 %collective-permute-start.1 = (s32[16,4]{1,0:T(8,128)S(1)}, s32[16,4]{1,0:T(8,128)}, u32[]{:S(2)}, u32[]{:S(2)}) collective-permute-start(s32[16,4]{1,0:T(8,128)S(1)} %copy.67), channel_id=1, source_target_pairs={{12,0},{0,4},{4,8},{8,12},{13,1},{1,5},{5,9},{9,13},{14,2},{2,6},{... | collective-permute-start | bytes 776 | tf_op jit(solution)/shard_map/while/body/eval_jaxpr/ppermute | solution.py:12
  127.9 3.6 %copy-start = (f32[16,64,4,64]{3,0,2,1:T(8,128)S(1)}, f32[16,64,4,64]{3,0,2,1:T(8,128)}, u32[]{:S(2)}) copy-start(f32[16,64,4,64]{3,0,2,1:T(8,128)} %get-tuple-element.140) | copy-start | bytes 3145732
where the time goes:
time: 137 us; the launch traced here: 135 us
  local copies, waits for them, and re-layouts  48.3 us (35%)
  waiting for transfers between devices  27.6 us (20%)
  starting transfers between devices  23 us (17%)
  matrix products  20.9 us (15%)
  other arithmetic  14.6 us (11%)
    ppermute x25, waiting for transfers between devices, from_behind(): return lax.ppermute(block, axis, route)  27.6 us
    ppermute x25, starting transfers between devices, from_behind(): return lax.ppermute(block, axis, route)  23 us
    dot_general x4, matrix products, contribute(): jnp.einsum('rs,sxmk->rxmk', owners, products, precision=lax.Precision.HIG...  15 us
    while x15, local copies, waits for them, and re-layouts  12.5 us
    gather x11, local copies, waits for them, and re-layouts, contribute(): b_values.reshape(row_count * offer_count, BS * BS)  9.94 us
    dot_general x3, local copies, waits for them, and re-layouts, contribute(): jnp.einsum('sxj,smjk->sxmk', left_blocks, picked.reshape(slot_total, kept...  9.33 us
    dot_general x4, matrix products, contribute(): jnp.einsum('sxj,smjk->sxmk', left_blocks, picked.reshape(slot_total, kept...  5.88 us
    select_n x5, other arithmetic, shards(): jnp.where(expand_like(taking, old_part), new_part, old_part)  3.38 us
  transfers between devices with their start and end apart: 25, of which 4 were waited for; matrix products, arithmetic and copies ran while one was open for 49% of the time, Pallas kernels for 0%

commit v1 on v0

v1 whole, which is shorter than its diff:
```python
import functools

import jax
import jax.numpy as jnp
from jax import lax
from jax.experimental import pallas as pl
from jax.experimental.pallas import tpu as pltpu
from jax.sharding import PartitionSpec as P

BS = 64
LANES = 128
ROWS = BS * BS // LANES
CAPACITY = 16
UNROLL = 4
IDLE = 63
VMEM = pltpu.VMEM
SMEM = pltpu.SMEM
BF16 = jnp.bfloat16
F32 = jnp.float32
I32 = jnp.int32


def shifted(block, axis, distance):
    size = lax.axis_size(axis)
    route = [(i, (i + distance) % size) for i in range(size)]
    return lax.ppermute(block, axis, route)


def prepare_kernel(a_ref, b_ref, a_out, b_out, a_wide, b_wide):
    source = lax.broadcasted_iota(I32, (LANES, LANES), 0)
    target = lax.broadcasted_iota(I32, (LANES, LANES), 1)
    wanted = (target // BS) * BS + 2 * (target % ROWS) + (target // ROWS) % 2
    order = (source == wanted).astype(BF16)
    for t in range(ROWS):
        piece = a_ref[0, :, pl.ds(t * LANES, LANES)]
        a_wide[:, t, :] = jnp.dot(piece, order, preferred_element_type=F32)
    a_out[...] = a_wide[...].astype(BF16)
    row_count, slots = b_ref.shape[0], b_ref.shape[1]

    def one_row(k, carry):
        for t in range(ROWS):
            b_wide[pl.ds(t * slots, slots), :] = b_ref[k, :, pl.ds(t * LANES, LANES)].astype(F32)
        for n in range(slots):
            b_out[k * slots + n] = b_wide[pl.ds(n, ROWS, stride=slots), :].astype(BF16)
        return carry

    lax.fori_loop(0, row_count, one_row, 0)


def prepare(a_blocks, b_blocks):
    slots = a_blocks.shape[1]
    blocks = b_blocks.shape[0] * b_blocks.shape[1]
    return pl.pallas_call(
        prepare_kernel,
        out_shape=(
            jax.ShapeDtypeStruct((slots, ROWS, LANES), BF16),
            jax.ShapeDtypeStruct((blocks, ROWS, LANES), BF16),
        ),
        in_specs=[pl.BlockSpec(memory_space=VMEM)] * 2,
        out_specs=(pl.BlockSpec(memory_space=VMEM),) * 2,
        scratch_shapes=[
            VMEM((slots, ROWS, LANES), F32),
            VMEM((b_blocks.shape[1] * ROWS, LANES), F32),
        ],
        compiler_params=pltpu.CompilerParams(vmem_limit_bytes=24 << 20),
        cost_estimate=pl.CostEstimate(flops=1 << 24, bytes_accessed=2 << 20, transcendentals=0),
        name="prepare",
    )(a_blocks, b_blocks)


def offered_hits(i, wanted, offered):
    kept = [wanted(m, i) for m in range(len(offered[1]))]
    return [functools.reduce(jnp.logical_or, [o == w for w in kept]) for o in offered[0]], kept


def fetch(copies, sems):
    started = [
        pltpu.make_async_copy(source, target, sems.at[at])
        for at, (source, target) in enumerate(copies)
    ]
    for copy in started:
        copy.start()
    for copy in started:
        copy.wait()


def pack_kernel(first, peers, per_col, *refs):
    refs = list(refs)
    base_ref = None if first else refs.pop(0)
    c_refs = [refs.pop(0) for _ in range(peers)]
    a_refs = [refs.pop(0) for _ in range(peers)]
    b_cols, blocks = refs.pop(0), refs.pop(0)
    outs = [refs.pop(0) for _ in range(peers - 1)]
    most = refs.pop(0)
    c_s, a_s, b_s, chosen, seen, sems = refs
    row_count, slots = b_cols.shape[1], b_cols.shape[0]
    kept, a_slots = c_refs[0].shape[0], a_refs[0].shape[2]
    copies = [(c_refs[d], c_s.at[d]) for d in range(1, peers)]
    copies += [(a_refs[d], a_s.at[d]) for d in range(peers)]
    copies += [(b_cols, b_s)]
    fetch(copies, sems)
    base = 0 if first else base_ref[0]
    col_count = peers // per_col
    grid_row = lax.axis_index("row")
    grid_col = lax.axis_index("col")
    turn = grid_row % per_col * col_count + grid_col
    top = 0
    for d in range(1, peers):
        place = (turn - grid_row + d + peers) % peers
        for k in range(row_count):
            seen[k] = 0

        def one_slot(s, count, d=d, place=place):
            i = a_s[place, 0, 0, s]
            k = jnp.maximum(a_s[place, 1, 0, s], 0)
            safe = jnp.maximum(i, 0)
            kept_cols = [c_s[d, m, safe] for m in range(kept)]
            before = seen[k]
            after = before
            for n in range(slots):
                column = b_s[n, k]
                hit = functools.reduce(jnp.logical_or, [column == c for c in kept_cols])
                hit = hit & (i >= 0)
                fresh = hit & ((before >> n) & 1 == 0)
                chosen[count] = k * slots + n
                count = count + fresh.astype(I32)
                after = after | (hit.astype(I32) << n)
            seen[k] = after
            return count

        count = lax.fori_loop(0, a_slots, one_slot, jnp.int32(0))
        for x in range(outs[d - 1].shape[0]):
            index = jnp.where(base + x < count, chosen[base + x], 0)
            outs[d - 1][x] = blocks[index]
        top = jnp.maximum(top, count)
    most[0] = top


def pack(base, c_parts, a_parts, b_cols, blocks, per_col):
    peers = len(c_parts)
    slots, row_count = b_cols.shape
    first = base is None
    any_spec = pl.BlockSpec(memory_space=pl.ANY)
    smem_spec = pl.BlockSpec(memory_space=SMEM)
    vmem_spec = pl.BlockSpec(memory_space=VMEM)
    given = [] if first else [base]
    results = pl.pallas_call(
        functools.partial(pack_kernel, first, peers, per_col),
        out_shape=[jax.ShapeDtypeStruct((CAPACITY, ROWS, LANES), BF16)] * (peers - 1)
        + [jax.ShapeDtypeStruct((1,), I32)],
        in_specs=[smem_spec] * len(given) + [any_spec] * (2 * peers + 1) + [vmem_spec],
        out_specs=[vmem_spec] * (peers - 1) + [smem_spec],
        scratch_shapes=[
            SMEM((peers,) + c_parts[0].shape, I32),
            SMEM((peers,) + a_parts[0].shape, I32),
            SMEM(b_cols.shape, I32),
            SMEM((row_count * slots + CAPACITY + 1,), I32),
            SMEM((row_count,), I32),
            pltpu.SemaphoreType.DMA((2 * peers + 1,)),
        ],
        compiler_params=pltpu.CompilerParams(vmem_limit_bytes=24 << 20),
        cost_estimate=pl.CostEstimate(flops=1 << 20, bytes_accessed=1 << 20, transcendentals=0),
        name="pack",
    )(*given, *c_parts, *a_parts, b_cols, blocks)
    return results[:-1], results[-1]


def encode(a_slot, out, peer, place):
    return ((a_slot * 64 + out) * 64 + place) * 64 + peer


def list_kernel(peers, cols, per_col, most_items, *refs):
    refs = list(refs)
    a_refs = [refs.pop(0) for _ in range(cols)]
    b_refs = [refs.pop(0) for _ in range(peers)]
    c_ref = refs.pop(0)
    items, total = refs.pop(0), refs.pop(0)
    a_s, b_s, c_s, seen, places, sems = refs
    kept, row_count = c_ref.shape
    slots = b_refs[0].shape[0]
    a_slots = a_refs[0].shape[2] // per_col
    copies = [(a_refs[h], a_s.at[h]) for h in range(cols)]
    copies += [(b_refs[d], b_s.at[d]) for d in range(peers)]
    copies += [(c_ref, c_s)]
    fetch(copies, sems)
    grid_row = lax.axis_index("row")
    grid_col = lax.axis_index("col")

    def one_peer(d, length):
        group = (grid_row + d) % peers
        holder = (group // per_col - grid_col + cols) % cols
        part = group % per_col
        for k in range(row_count):
            seen[k] = 0

        def one_slot(s, state):
            length, count = state
            i = a_s[holder, 0, 0, part * a_slots + s]
            k = jnp.maximum(a_s[holder, 1, 0, part * a_slots + s], 0)
            safe = jnp.maximum(i, 0)
            kept_cols = [c_s[m, safe] for m in range(kept)]
            before = seen[k]
            after = before
            a_slot = (holder * per_col + part) * a_slots + s
            for n in range(slots):
                column = b_s[d, n, k]
                equal = [column == c for c in kept_cols]
                hit = functools.reduce(jnp.logical_or, equal) & (i >= 0)
                which = sum(m * e.astype(I32) for m, e in enumerate(equal))
                fresh = hit & ((before >> n) & 1 == 0)
                spot = k * slots + n
                place = jnp.where(fresh, count, places[spot])
                places[spot] = place
                stored = jnp.where(d == 0, spot, place)
                items[length] = encode(a_slot, safe * kept + which, d, stored)
                length = length + hit.astype(I32)
                count = count + fresh.astype(I32)
                after = after | (hit.astype(I32) << n)
            seen[k] = after
            return length, count

        length, _ = lax.fori_loop(0, a_slots, one_slot, (length, jnp.int32(0)))
        return length

    for spot in range(row_count * slots):
        places[spot] = 0
    length = lax.fori_loop(0, peers, one_peer, jnp.int32(0))
    for u in range(UNROLL):
        items[length + u] = IDLE
    total[0] = length


def work_list(a_parts, b_parts, c_cols, per_col):
    cols, peers = len(a_parts), len(b_parts)
    slots, row_count = b_parts[0].shape
    a_slots = a_parts[0].shape[2] // per_col
    most_items = peers * a_slots * slots + UNROLL + slots
    any_spec = pl.BlockSpec(memory_space=pl.ANY)
    smem_spec = pl.BlockSpec(memory_space=SMEM)
    return pl.pallas_call(
        functools.partial(list_kernel, peers, cols, per_col, most_items),
        out_shape=[
            jax.ShapeDtypeStruct((most_items,), I32),
            jax.ShapeDtypeStruct((1,), I32),
        ],
        in_specs=[any_spec] * (cols + peers + 1),
        out_specs=[smem_spec] * 2,
        scratch_shapes=[
            SMEM((cols,) + a_parts[0].shape, I32),
            SMEM((peers,) + b_parts[0].shape, I32),
            SMEM(c_cols.shape, I32),
            SMEM((row_count,), I32),
            SMEM((row_count * slots,), I32),
            pltpu.SemaphoreType.DMA((cols + peers + 1,)),
        ],
        cost_estimate=pl.CostEstimate(flops=1 << 20, bytes_accessed=1 << 16, transcendentals=0),
        name="work_list",
    )(*a_parts, *b_parts, c_cols)


def multiply_kernel(first, peers, cols, *refs):
    refs = list(refs)
    base_ref = previous = None
    if not first:
        base_ref, previous = refs.pop(0), refs.pop(0)
    items, total = refs.pop(0), refs.pop(0)
    a_refs = [refs.pop(0) for _ in range(cols)]
    own = refs.pop(0)
    b_refs = [refs.pop(0) for _ in range(peers - 1)]
    out = refs.pop(0)
    a_v, b_v, sums, sems = refs
    held, own_count = a_refs[0].shape[0], own.shape[0]
    row_count, kept = out.shape[0], out.shape[1]
    copies = [(a_refs[h], a_v.at[pl.ds(h * held, held)]) for h in range(cols)]
    copies += [(own, b_v.at[pl.ds(0, own_count)])]
    copies += [
        (b_refs[d], b_v.at[pl.ds(own_count + d * CAPACITY, CAPACITY)]) for d in range(peers - 1)
    ]
    started = [
        pltpu.make_async_copy(source, target, sems.at[at])
        for at, (source, target) in enumerate(copies)
    ]
    for copy in started:
        copy.start()
    sums[...] = jnp.zeros_like(sums)
    for copy in started:
        copy.wait()
    base = 0 if first else base_ref[0]
    low = lax.broadcasted_iota(I32, (ROWS, LANES), 1) < BS
    nothing = jnp.zeros((ROWS, LANES), BF16)

    def some_items(step, carry):
        for u in range(UNROLL):
            word = items[step * UNROLL + u]
            peer = word & 63
            place = (word >> 6) & 63
            target = (word >> 12) & 63
            a_slot = word >> 18
            inside = (place >= base) & (place < base + CAPACITY)
            own_item = peer == 0
            used = (inside & (peer > 0) & (peer < IDLE)) | (own_item if first else False)
            spot = jnp.where(own_item, place, own_count + (peer - 1) * CAPACITY + place - base)
            spot = jnp.where(used, spot, 0)
            left = a_v[a_slot]
            block = b_v[spot]
            turned = jnp.concatenate([block[:, BS:], block[:, :BS]], axis=1)
            right = jnp.concatenate(
                [
                    jnp.where(low, block, nothing),
                    jnp.where(low, turned, nothing),
                    jnp.where(low, nothing, turned),
                    jnp.where(low, nothing, block),
                ],
                axis=0,
            )
            term = jnp.dot(left, right, preferred_element_type=F32)
            i = jnp.where(used, target // kept, row_count)
            m = target % kept
            sums[i, pl.ds(m, ROWS, stride=kept), :] += term
        return carry

    lax.fori_loop(0, (total[0] + UNROLL - 1) // UNROLL, some_items, 0)

    def one_row(i, carry):
        for t in range(ROWS):
            piece = sums[i, pl.ds(t * kept, kept), :]
            if previous is not None:
                piece = piece + previous[i, :, pl.ds(t * LANES, LANES)]
            out[i, :, pl.ds(t * LANES, LANES)] = piece
        return carry

    lax.fori_loop(0, row_count, one_row, 0)


def multiply(base, previous, items, total, a_parts, own, b_parts, shape):
    first = base is None
    cols, peers = len(a_parts), len(b_parts) + 1
    any_spec = pl.BlockSpec(memory_space=pl.ANY)
    smem_spec = pl.BlockSpec(memory_space=SMEM)
    vmem_spec = pl.BlockSpec(memory_space=VMEM)
    given = [] if first else [base, previous]
    specs = [] if first else [smem_spec, vmem_spec]
    held = a_parts[0].shape[0]
    stored = own.shape[0] + (peers - 1) * CAPACITY
    return pl.pallas_call(
        functools.partial(multiply_kernel, first, peers, cols),
        out_shape=jax.ShapeDtypeStruct(shape, F32),
        in_specs=specs + [smem_spec] * 2 + [any_spec] * (cols + peers),
        out_specs=vmem_spec,
        scratch_shapes=[
            VMEM((cols * held, ROWS, LANES), BF16),
            VMEM((stored, ROWS, LANES), BF16),
            VMEM((shape[0] + 1, ROWS * shape[1], LANES), F32),
            pltpu.SemaphoreType.DMA((cols + peers,)),
        ],
        compiler_params=pltpu.CompilerParams(vmem_limit_bytes=32 << 20),
        cost_estimate=pl.CostEstimate(flops=1 << 26, bytes_accessed=4 << 20, transcendentals=0),
        name="multiply",
    )(*given, items, total, *a_parts, own, *b_parts)


def send_rows(parts):
    return [shifted(part, "row", -(d + 1)) for d, part in enumerate(parts)]


def index_parts(a_index, rows, cols, per_col):
    count = a_index.shape[2] // per_col
    grid_row = lax.axis_index("row")
    parts = []
    for d in range(rows):
        route = []
        for r in range(rows):
            for c in range(cols):
                turn = (r + d) % rows
                target = (c * per_col + turn // cols) * cols + turn % cols
                route.append((r * cols + c, target))
        mine = a_index
        if per_col > 1:
            turn = (grid_row + d) % rows
            mine = lax.dynamic_slice_in_dim(a_index, turn // cols * count, count, axis=2)
        parts.append(lax.ppermute(mine, ("row", "col"), route))
    return parts


def shards(a_blocks, a_index, b_blocks, b_cols, c_cols):
    rows = lax.axis_size("row")
    cols = lax.axis_size("col")
    per_col = rows // cols
    b_turned = b_cols.T
    c_turned = c_cols.T
    c_parts = [c_turned] + [shifted(c_turned, "row", d) for d in range(1, rows)]
    a_near = index_parts(a_index, rows, cols, per_col)
    a_ready, own = prepare(a_blocks, b_blocks)
    a_far = [a_index] + [shifted(a_index, "col", -h) for h in range(1, cols)]
    b_parts = [b_turned] + [shifted(b_turned, "row", -d) for d in range(1, rows)]
    a_parts = [a_ready] + [shifted(a_ready, "col", -h) for h in range(1, cols)]

    packed, most = pack(None, c_parts, a_near, b_turned, own, per_col)
    arrived = send_rows(packed)
    rounds = (lax.pmax(most[0], ("sys", "row", "col")) + CAPACITY - 1) // CAPACITY
    items, total = work_list(a_far, b_parts, c_turned, per_col)
    shape = (b_blocks.shape[0], c_cols.shape[1], BS * BS)
    sums = multiply(None, None, items, total, a_parts, own, arrived, shape)

    def more(state):
        return state[0] < rounds

    def one_round(state):
        at, sums = state
        base = jnp.reshape(at * CAPACITY, (1,))
        packed, _ = pack(base, c_parts, a_near, b_turned, own, per_col)
        arrived = send_rows(packed)
        sums = multiply(base, sums, items, total, a_parts, own, arrived, shape)
        return at + 1, sums

    return lax.while_loop(more, one_round, (jnp.int32(1), sums))[1]


def solution(mesh):
    return jax.shard_map(
        shards,
        mesh=mesh,
        in_specs=(
            P(("sys", "row"), "col", None),
            P(None, ("sys", "row"), "col"),
            P(("sys", "row"), "col", None),
            P(("sys", "row"), "col"),
            P(("sys", "row"), "col"),
        ),
        out_specs=P(("sys", "row"), "col", None),
        check_vma=False,
    )
```

time: 137 us -> 89.9 us (0.66); the launches traced: 135 us -> 89.6 us
  local copies, waits for them, and re-layouts: 48.3 us -> 2.95 us
  blocking collectives: 0 us -> 41.3 us
  waiting for transfers between devices: 27.6 us -> 2.06 us
  matrix products: 20.9 us -> 0 us
  Pallas kernels: 0 us -> 15.4 us
  other arithmetic: 14.6 us -> 0 us
  starting transfers between devices: 23 us -> 27.1 us
    pmax x0 -> x1, blocking collectives: none -> 41.3 us  [shards(): lax.pmax(most[0], ('sys', 'row', 'col')) + CAPACITY - 1]
    ppermute x25 -> x19, waiting for transfers between devices: 27.6 us -> 2.06 us  [the longest x15 2.05 us: shifted(): return lax.ppermute(block, axis, route)]
    dot_general x8 -> x0, matrix products: 20.9 us -> none  [the longest x4 15 us: contribute(): jnp.einsum('rs,sxmk->rxmk', owners, products, precision=lax.Precision.HIG...]
    gather x28 -> x0, local copies, waits for them, and re-layouts: 16.5 us -> none  [the longest x11 9.94 us: contribute(): b_values.reshape(row_count * offer_count, BS * BS)]
    pallas_call x0 -> x4, Pallas kernels: none -> 15.4 us  [the longest x1 6.65 us: work_list(): pl.pallas_call(functools.partial(list_kernel, peers, cols, per_col, most_...]
    while x15 -> x0, local copies, waits for them, and re-layouts: 12.5 us -> none
    dot_general x3 -> x0, local copies, waits for them, and re-layouts: 9.33 us -> none  [contribute(): jnp.einsum('sxj,smjk->sxmk', left_blocks, picked.reshape(slot_total, kept...]
    select_n x17 -> x0, other arithmetic: 7.67 us -> none  [the longest x5 3.38 us: shards(): jnp.where(expand_like(taking, old_part), new_part, old_part)]
  transfers between devices with their start and end apart: 25 -> 19, of which waited for: 4 -> 2; matrix products, arithmetic and copies ran while one was open for 49% -> 0% of each run, Pallas kernels for 0% -> 11%
where the time goes in v1:
time: 89.9 us; the launch traced here: 89.6 us
  blocking collectives  41.3 us (46%)
  starting transfers between devices  27.1 us (30%)
  Pallas kernels  15.4 us (17%)
  local copies, waits for them, and re-layouts  2.95 us (3%)
  waiting for transfers between devices  2.06 us (2%)
    pmax x1, blocking collectives, shards(): lax.pmax(most[0], ('sys', 'row', 'col')) + CAPACITY - 1  41.3 us
    ppermute x15, starting transfers between devices, shifted(): return lax.ppermute(block, axis, route)  18.2 us
    ppermute x4, starting transfers between devices, index_parts(): parts.append(lax.ppermute(mine, ('row', 'col'), route))  8.96 us
    pallas_call x1, Pallas kernels, work_list(): pl.pallas_call(functools.partial(list_kernel, peers, cols, per_col, most_...  6.65 us
    pallas_call x1, Pallas kernels, multiply(): pl.pallas_call(functools.partial(multiply_kernel, first, peers, cols), ou...  4.5 us
    pallas_call x1, Pallas kernels, pack(): pl.pallas_call(functools.partial(pack_kernel, first, peers, per_col), out...  3.54 us
    unnamed x24, local copies, waits for them, and re-layouts  2.95 us
    ppermute x15, waiting for transfers between devices, shifted(): return lax.ppermute(block, axis, route)  2.05 us
  transfers between devices with their start and end apart: 19, of which 2 were waited for; matrix products, arithmetic and copies ran while one was open for 0% of the time, Pallas kernels for 11%

profile of v1, /device:TPU:0, one launch (start us, length us, event | category | flops | bytes accessed | tf_op | source)
XLA Modules:
  0.0 89.6 jit_solution(11010460111326691895)
XLA Ops:
  0.0 1.0 %copy-done = bf16[16,4,4096]{2,1,0:T(4,128)(2,1)S(1)} copy-done((bf16[16,4,4096]{2,1,0:T(4,128)(2,1)S(1)}, bf16[16,4,4096]{2,1,0:T(4,128)(2,1)}, u32[]{:S(2)}) %copy-start) | copy-done | bytes 524312
  1.0 0.9 %copy-done.1 = bf16[1,16,4096]{2,1,0:T(8,128)(2,1)S(1)} copy-done((bf16[1,16,4096]{2,1,0:T(8,128)(2,1)S(1)}, bf16[1,16,4096]{2,1,0:T(8,128)(2,1)}, u32[]{:S(2)}) %copy-start.1) | copy-done | bytes 131096
  1.9 0.7 prepare.1
  2.7 0.0 copy-start.4
  2.7 0.5 collective-permute-start.11
  3.2 2.6 %collective-permute-start.16 = (s32[2,1,16]{2,1,0:T(1,128)S(1)}, s32[2,1,16]{2,1,0:T(1,128)S(1)}, u32[]{:S(2)}, u32[]{:S(2)}) collective-permute-start(s32[2,1,16]{2,1,0:T(1,128)S(1)} %copy-done.8), channel_id=1, source_target_pairs={{0,1},{1,5},{2,9},{3,13},{4,2},{5,6},{6,10},{7,14},{8,3},{9,7},{10... | collective-permute-start | bytes 392 | tf_op jit(solution)/shard_map/ppermute | solution.py:381
  5.8 0.6 collective-permute-start.15
  6.5 5.7 %collective-permute-start.18 = (s32[2,1,16]{2,1,0:T(1,128)S(1)}, s32[2,1,16]{2,1,0:T(1,128)S(1)}, u32[]{:S(2)}, u32[]{:S(2)}) collective-permute-start(s32[2,1,16]{2,1,0:T(1,128)S(1)} %copy-done.8), channel_id=1, source_target_pairs={{0,3},{1,7},{2,11},{3,15},{4,0},{5,4},{6,8},{7,12},{8,1},{9,5},{10... | collective-permute-start | bytes 392 | tf_op jit(solution)/shard_map/ppermute | solution.py:381
  12.2 0.0 collective-permute-start.17
  12.2 0.0 collective-permute-done.16.refs_5_
  12.2 0.0 copy-start.3
  12.2 3.6 %collective-permute-start.14 = (s32[4,16]{1,0:T(4,128)S(1)}, s32[4,16]{1,0:T(4,128)S(1)}, u32[]{:S(2)}, u32[]{:S(2)}) collective-permute-start(s32[4,16]{1,0:T(4,128)S(1)} %bitcast.12), channel_id=1, source_target_pairs={{0,12},{4,0},{8,4},{12,8},{1,13},{5,1},{9,5},{13,9},{2,14},{6,2},{... | collective-permute-start | bytes 776 | tf_op jit(solution)/shard_map/ppermute | solution.py:26
  15.8 0.0 collective-permute-done.18.refs_7_
  15.8 1.4 %collective-permute-start.12 = (s32[4,16]{1,0:T(4,128)S(1)}, s32[4,16]{1,0:T(4,128)S(1)}, u32[]{:S(2)}, u32[]{:S(2)}) collective-permute-start(s32[4,16]{1,0:T(4,128)S(1)} %bitcast.14), channel_id=1, source_target_pairs={{0,4},{4,8},{8,12},{12,0},{1,5},{5,9},{9,13},{13,1},{2,6},{6,10},{... | collective-permute-start | bytes 776 | tf_op jit(solution)/shard_map/ppermute | solution.py:26
  17.2 1.1 %collective-permute-start.5 = (s32[2,1,16]{2,1,0:T(1,128)S(1)}, s32[2,1,16]{2,1,0:T(1,128)S(1)}, u32[]{:S(2)}, u32[]{:S(2)}) collective-permute-start(s32[2,1,16]{2,1,0:T(1,128)S(1)} %copy-done.8), channel_id=1, source_target_pairs={{0,1},{1,2},{2,3},{3,0},{4,5},{5,6},{6,7},{7,4},{8,9},{9,10},{10,1... | collective-permute-start | bytes 392 | tf_op jit(solution)/shard_map/ppermute | solution.py:26
  18.3 0.6 collective-permute-start.4
  18.9 1.3 %collective-permute-done.13.refs_2_ = s32[4,16]{1,0:T(4,128)S(1)} collective-permute-done((s32[4,16]{1,0:T(4,128)S(1)}, s32[4,16]{1,0:T(4,128)S(1)}, u32[]{:S(2)}, u32[]{:S(2)}) %collective-permute-start.13) | collective-permute-done | bytes 288 | tf_op jit(solution)/shard_map/ppermute | solution.py:26
  20.3 0.9 collective-permute-start.3
  21.1 0.7 collective-permute-done.12.refs_1_
  21.8 3.5 %pack.2 = (bf16[16,32,128]{2,1,0:T(8,128)(2,1)S(1)}, bf16[16,32,128]{2,1,0:T(8,128)(2,1)S(1)}, bf16[16,32,128]{2,1,0:T(8,128)(2,1)S(1)}, s32[1]{0:T(128)}) custom-call(s32[4,16]{1,0:T(4,128)S(1)} %bitcast.15, s32[4,16]{1,0:T(4,128)S(1)} %collective-permute-done.12.refs_1_, s32[4,16]{1,0:T(4,128)S(1)} %collective-permute-done.13.refs_2_, ...), custom_call_target="tpu_custom_call" | custom-call | flops 1048576 | bytes 1048576 | tf_op jit(solution)/shard_map/pack/pallas_call | solution.py:147
  25.4 0.1 collective-permute-start.8
  25.4 2.6 %collective-permute-start.7 = (s32[4,16]{1,0:T(4,128)S(1)}, s32[4,16]{1,0:T(4,128)S(1)}, u32[]{:S(2)}, u32[]{:S(2)}) collective-permute-start(s32[4,16]{1,0:T(4,128)S(1)} %bitcast.8), channel_id=1, source_target_pairs={{0,8},{4,12},{8,0},{12,4},{1,9},{5,13},{9,1},{13,5},{2,10},{6,14},... | collective-permute-start | bytes 776 | tf_op jit(solution)/shard_map/ppermute | solution.py:26
  28.0 1.3 %collective-permute-start.6 = (s32[4,16]{1,0:T(4,128)S(1)}, s32[4,16]{1,0:T(4,128)S(1)}, u32[]{:S(2)}, u32[]{:S(2)}) collective-permute-start(s32[4,16]{1,0:T(4,128)S(1)} %bitcast.9), channel_id=1, source_target_pairs={{0,12},{4,0},{8,4},{12,8},{1,13},{5,1},{9,5},{13,9},{2,14},{6,2},{... | collective-permute-start | bytes 776 | tf_op jit(solution)/shard_map/ppermute | solution.py:26
  29.3 2.0 %collective-permute-start.10 = (bf16[16,32,128]{2,1,0:T(8,128)(2,1)S(1)}, bf16[16,32,128]{2,1,0:T(8,128)(2,1)S(1)}, u32[]{:S(2)}, u32[]{:S(2)}) collective-permute-start(bf16[16,32,128]{2,1,0:T(8,128)(2,1)S(1)} %get-tuple-element.298.refs_2_), channel_id=1, source_target_pairs={{0,2},{1,3},{2,0},{3,1},{4,6},{5,7},{6,4},{7,5},{8,10},{9,11},{10,... | collective-permute-start | bytes 393224 | tf_op jit(solution)/shard_map/ppermute | solution.py:26
  31.4 2.3 %collective-permute-start.19 = (bf16[16,32,128]{2,1,0:T(8,128)(2,1)S(1)}, bf16[16,32,128]{2,1,0:T(8,128)(2,1)S(1)}, u32[]{:S(2)}, u32[]{:S(2)}) collective-permute-start(bf16[16,32,128]{2,1,0:T(8,128)(2,1)S(1)} %get-tuple-element.118), channel_id=1, source_target_pairs={{0,12},{4,0},{8,4},{12,8},{1,13},{5,1},{9,5},{13,9},{2,14},{6,2},{... | collective-permute-start | bytes 393224 | tf_op jit(solution)/shard_map/ppermute | solution.py:26
  33.7 0.1 collective-permute-start.20
  33.8 1.7 %collective-permute-start.21 = (bf16[16,32,128]{2,1,0:T(8,128)(2,1)S(1)}, bf16[16,32,128]{2,1,0:T(8,128)(2,1)S(1)}, u32[]{:S(2)}, u32[]{:S(2)}) collective-permute-start(bf16[16,32,128]{2,1,0:T(8,128)(2,1)S(1)} %get-tuple-element.120), channel_id=1, source_target_pairs={{0,4},{4,8},{8,12},{12,0},{1,5},{5,9},{9,13},{13,1},{2,6},{6,10},{... | collective-permute-start | bytes 393224 | tf_op jit(solution)/shard_map/ppermute | solution.py:26
  35.6 41.3 %pmax.7 = s32[]{:T(128)} all-reduce(s32[]{:T(128)} %bitcast.3), channel_id=1, replica_groups=mesh['sys'=2,'row'=4,'col'=4] {'sys','row','col'}, use_global_device_ids=true, to_apply=%region_0.0 | all-reduce | flops 1 | bytes 8 | tf_op jit(solution)/shard_map/pmax | solution.py:400
  77.4 6.6 %work_list.1 = (s32[264]{0:T(512)S(1)}, s32[1]{0:T(128)}) custom-call(s32[2,1,16]{2,1,0:T(1,128)} %refs_0_.1, s32[2,1,16]{2,1,0:T(1,128)} %copy-done.11, s32[2,1,16]{2,1,0:T(1,128)} %copy-done.10, s32[2,1,16]{2,1,0:T(1,128)} %copy-done.9, s32[4,16]{1,0:T(4,128)S(1)} %bitcast.10, s32[4,16]{1,0:T(4,128)} %copy-done.7, s32[4,16]{1,0:T(4,128)} %copy-done.6, ...), custom_call_target="tpu_custom_call" | custom-call | flops 1048576 | bytes 65536 | tf_op jit(solution)/shard_map/work_list/pallas_call | solution.py:240
  84.1 4.5 %multiply.2 = f32[16,4,4096]{2,1,0:T(4,128)S(1)} custom-call(s32[264]{0:T(512)S(1)} %get-tuple-element.296.refs_0_, s32[1]{0:T(128)} %get-tuple-element.297.refs_1_, bf16[16,32,128]{2,1,0:T(8,128)(2,1)S(1)} %get-tuple-element.298.refs_2_, bf16[16,32,128]{2,1,0:T(8,128)(2,1)S(1)} %collective-permute-done.9.refs_3_, ...), custom_call_target="tpu_custom_call" | custom-call | flops 67108864 | bytes 4194304 | tf_op jit(solution)/shard_map/multiply/pallas_call | solution.py:345
  88.7 0.0 copy-start.2
  88.7 1.0 %copy-done.2 = f32[16,4,4096]{2,1,0:T(4,128)} copy-done((f32[16,4,4096]{2,1,0:T(4,128)}, f32[16,4,4096]{2,1,0:T(4,128)S(1)}, u32[]{:S(2)}) %copy-start.2) | copy-done | bytes 1048600
  (36 shorter events, 0.1 us)
Async XLA Ops:
  0.0 1.0 %copy-start = (bf16[16,4,4096]{2,1,0:T(4,128)(2,1)S(1)}, bf16[16,4,4096]{2,1,0:T(4,128)(2,1)}, u32[]{:S(2)}) copy-start(bf16[16,4,4096]{2,1,0:T(4,128)(2,1)} %b_ref.1) | copy-start | bytes 1572868
  1.0 0.9 %copy-start.1 = (bf16[1,16,4096]{2,1,0:T(8,128)(2,1)S(1)}, bf16[1,16,4096]{2,1,0:T(8,128)(2,1)}, u32[]{:S(2)}) copy-start(bf16[1,16,4096]{2,1,0:T(8,128)(2,1)} %a_ref.1) | copy-start | bytes 393220
  1.9 1.3 %copy-start.8 = (s32[2,1,16]{2,1,0:T(1,128)S(1)}, s32[2,1,16]{2,1,0:T(1,128)}, u32[]{:S(2)}) copy-start(s32[2,1,16]{2,1,0:T(1,128)} %refs_0_.1) | copy-start | bytes 388
  2.7 9.5 %copy-start.4 = (s32[16,4]{0,1:T(4,128)S(1)}, s32[16,4]{0,1:T(4,128)}, u32[]{:S(2)}) copy-start(s32[16,4]{0,1:T(4,128)} %param.11) | copy-start | bytes 772
  2.7 31.1 %collective-permute-start.11 = (bf16[16,32,128]{2,1,0:T(8,128)(2,1)S(1)}, bf16[16,32,128]{2,1,0:T(8,128)(2,1)S(1)}, u32[]{:S(2)}, u32[]{:S(2)}) collective-permute-start(bf16[16,32,128]{2,1,0:T(8,128)(2,1)S(1)} %get-tuple-element.298.refs_2_), channel_id=1, source_target_pairs={{0,1},{1,2},{2,3},{3,0},{4,5},{5,6},{6,7},{7,4},{8,9},{9,10},{10,1... | collective-permute-start | bytes 393224 | tf_op jit(solution)/shard_map/ppermute | solution.py:26
  3.2 9.0 %collective-permute-start.16 = (s32[2,1,16]{2,1,0:T(1,128)S(1)}, s32[2,1,16]{2,1,0:T(1,128)S(1)}, u32[]{:S(2)}, u32[]{:S(2)}) collective-permute-start(s32[2,1,16]{2,1,0:T(1,128)S(1)} %copy-done.8), channel_id=1, source_target_pairs={{0,1},{1,5},{2,9},{3,13},{4,2},{5,6},{6,10},{7,14},{8,3},{9,7},{10... | collective-permute-start | bytes 392 | tf_op jit(solution)/shard_map/ppermute | solution.py:381
  5.8 10.0 %collective-permute-start.15 = (s32[2,1,16]{2,1,0:T(1,128)S(1)}, s32[2,1,16]{2,1,0:T(1,128)S(1)}, u32[]{:S(2)}, u32[]{:S(2)}) collective-permute-start(s32[2,1,16]{2,1,0:T(1,128)S(1)} %copy-done.8), channel_id=1, source_target_pairs={{0,0},{1,4},{2,8},{3,12},{4,1},{5,5},{6,9},{7,13},{8,2},{9,6},{10,... | collective-permute-start | bytes 392 | tf_op jit(solution)/shard_map/ppermute | solution.py:381
  6.5 9.3 %collective-permute-start.18 = (s32[2,1,16]{2,1,0:T(1,128)S(1)}, s32[2,1,16]{2,1,0:T(1,128)S(1)}, u32[]{:S(2)}, u32[]{:S(2)}) collective-permute-start(s32[2,1,16]{2,1,0:T(1,128)S(1)} %copy-done.8), channel_id=1, source_target_pairs={{0,3},{1,7},{2,11},{3,15},{4,0},{5,4},{6,8},{7,12},{8,1},{9,5},{10... | collective-permute-start | bytes 392 | tf_op jit(solution)/shard_map/ppermute | solution.py:381
  12.2 5.1 %collective-permute-start.17 = (s32[2,1,16]{2,1,0:T(1,128)S(1)}, s32[2,1,16]{2,1,0:T(1,128)S(1)}, u32[]{:S(2)}, u32[]{:S(2)}) collective-permute-start(s32[2,1,16]{2,1,0:T(1,128)S(1)} %copy-done.8), channel_id=1, source_target_pairs={{0,2},{1,6},{2,10},{3,14},{4,3},{5,7},{6,11},{7,15},{8,0},{9,4},{1... | collective-permute-start | bytes 392 | tf_op jit(solution)/shard_map/ppermute | solution.py:381
  12.2 9.6 %copy-start.3 = (s32[16,4]{0,1:T(4,128)S(1)}, s32[16,4]{0,1:T(4,128)}, u32[]{:S(2)}) copy-start(s32[16,4]{0,1:T(4,128)} %param.10) | copy-start | bytes 772
  12.2 6.1 %collective-permute-start.14 = (s32[4,16]{1,0:T(4,128)S(1)}, s32[4,16]{1,0:T(4,128)S(1)}, u32[]{:S(2)}, u32[]{:S(2)}) collective-permute-start(s32[4,16]{1,0:T(4,128)S(1)} %bitcast.12), channel_id=1, source_target_pairs={{0,12},{4,0},{8,4},{12,8},{1,13},{5,1},{9,5},{13,9},{2,14},{6,2},{... | collective-permute-start | bytes 776 | tf_op jit(solution)/shard_map/ppermute | solution.py:26
  15.8 4.5 %collective-permute-start.13 = (s32[4,16]{1,0:T(4,128)S(1)}, s32[4,16]{1,0:T(4,128)S(1)}, u32[]{:S(2)}, u32[]{:S(2)}) collective-permute-start(s32[4,16]{1,0:T(4,128)S(1)} %bitcast.13), channel_id=1, source_target_pairs={{0,8},{4,12},{8,0},{12,4},{1,9},{5,13},{9,1},{13,5},{2,10},{6,14},... | collective-permute-start | bytes 776 | tf_op jit(solution)/shard_map/ppermute | solution.py:26
  15.8 6.0 %collective-permute-start.12 = (s32[4,16]{1,0:T(4,128)S(1)}, s32[4,16]{1,0:T(4,128)S(1)}, u32[]{:S(2)}, u32[]{:S(2)}) collective-permute-start(s32[4,16]{1,0:T(4,128)S(1)} %bitcast.14), channel_id=1, source_target_pairs={{0,4},{4,8},{8,12},{12,0},{1,5},{5,9},{9,13},{13,1},{2,6},{6,10},{... | collective-permute-start | bytes 776 | tf_op jit(solution)/shard_map/ppermute | solution.py:26
  17.2 8.2 %collective-permute-start.5 = (s32[2,1,16]{2,1,0:T(1,128)S(1)}, s32[2,1,16]{2,1,0:T(1,128)S(1)}, u32[]{:S(2)}, u32[]{:S(2)}) collective-permute-start(s32[2,1,16]{2,1,0:T(1,128)S(1)} %copy-done.8), channel_id=1, source_target_pairs={{0,1},{1,2},{2,3},{3,0},{4,5},{5,6},{6,7},{7,4},{8,9},{9,10},{10,1... | collective-permute-start | bytes 392 | tf_op jit(solution)/shard_map/ppermute | solution.py:26
  18.3 9.7 %collective-permute-start.4 = (s32[2,1,16]{2,1,0:T(1,128)S(1)}, s32[2,1,16]{2,1,0:T(1,128)S(1)}, u32[]{:S(2)}, u32[]{:S(2)}) collective-permute-start(s32[2,1,16]{2,1,0:T(1,128)S(1)} %copy-done.8), channel_id=1, source_target_pairs={{0,2},{1,3},{2,0},{3,1},{4,6},{5,7},{6,4},{7,5},{8,10},{9,11},{10,... | collective-permute-start | bytes 392 | tf_op jit(solution)/shard_map/ppermute | solution.py:26
  20.3 9.1 %collective-permute-start.3 = (s32[2,1,16]{2,1,0:T(1,128)S(1)}, s32[2,1,16]{2,1,0:T(1,128)S(1)}, u32[]{:S(2)}, u32[]{:S(2)}) collective-permute-start(s32[2,1,16]{2,1,0:T(1,128)S(1)} %copy-done.8), channel_id=1, source_target_pairs={{0,3},{1,0},{2,1},{3,2},{4,7},{5,4},{6,5},{7,6},{8,11},{9,8},{10,9... | collective-permute-start | bytes 392 | tf_op jit(solution)/shard_map/ppermute | solution.py:26
  25.4 6.0 %collective-permute-start.8 = (s32[4,16]{1,0:T(4,128)S(1)}, s32[4,16]{1,0:T(4,128)S(1)}, u32[]{:S(2)}, u32[]{:S(2)}) collective-permute-start(s32[4,16]{1,0:T(4,128)S(1)} %bitcast.7), channel_id=1, source_target_pairs={{0,4},{4,8},{8,12},{12,0},{1,5},{5,9},{9,13},{13,1},{2,6},{6,10},{... | collective-permute-start | bytes 776 | tf_op jit(solution)/shard_map/ppermute | solution.py:26
  25.4 8.3 %copy-start.9 = (s32[2,1,16]{2,1,0:T(1,128)}, s32[2,1,16]{2,1,0:T(1,128)S(1)}, u32[]{:S(2)}) copy-start(s32[2,1,16]{2,1,0:T(1,128)S(1)} %collective-permute-done.5.refs_3_) | copy-start | bytes 388
  25.4 5.9 %collective-permute-start.7 = (s32[4,16]{1,0:T(4,128)S(1)}, s32[4,16]{1,0:T(4,128)S(1)}, u32[]{:S(2)}, u32[]{:S(2)}) collective-permute-start(s32[4,16]{1,0:T(4,128)S(1)} %bitcast.8), channel_id=1, source_target_pairs={{0,8},{4,12},{8,0},{12,4},{1,9},{5,13},{9,1},{13,5},{2,10},{6,14},... | collective-permute-start | bytes 776 | tf_op jit(solution)/shard_map/ppermute | solution.py:26
  28.0 7.6 %copy-start.10 = (s32[2,1,16]{2,1,0:T(1,128)}, s32[2,1,16]{2,1,0:T(1,128)S(1)}, u32[]{:S(2)}) copy-start(s32[2,1,16]{2,1,0:T(1,128)S(1)} %collective-permute-done.4.refs_2_) | copy-start | bytes 388
  28.0 5.7 %collective-permute-start.6 = (s32[4,16]{1,0:T(4,128)S(1)}, s32[4,16]{1,0:T(4,128)S(1)}, u32[]{:S(2)}, u32[]{:S(2)}) collective-permute-start(s32[4,16]{1,0:T(4,128)S(1)} %bitcast.9), channel_id=1, source_target_pairs={{0,12},{4,0},{8,4},{12,8},{1,13},{5,1},{9,5},{13,9},{2,14},{6,2},{... | collective-permute-start | bytes 776 | tf_op jit(solution)/shard_map/ppermute | solution.py:26
  29.3 6.2 %copy-start.11 = (s32[2,1,16]{2,1,0:T(1,128)}, s32[2,1,16]{2,1,0:T(1,128)S(1)}, u32[]{:S(2)}) copy-start(s32[2,1,16]{2,1,0:T(1,128)S(1)} %collective-permute-done.3.refs_1_) | copy-start | bytes 388
  29.3 54.8 %collective-permute-start.10 = (bf16[16,32,128]{2,1,0:T(8,128)(2,1)S(1)}, bf16[16,32,128]{2,1,0:T(8,128)(2,1)S(1)}, u32[]{:S(2)}, u32[]{:S(2)}) collective-permute-start(bf16[16,32,128]{2,1,0:T(8,128)(2,1)S(1)} %get-tuple-element.298.refs_2_), channel_id=1, source_target_pairs={{0,2},{1,3},{2,0},{3,1},{4,6},{5,7},{6,4},{7,5},{8,10},{9,11},{10,... | collective-permute-start | bytes 393224 | tf_op jit(solution)/shard_map/ppermute | solution.py:26
  31.4 2.5 %copy-start.5 = (s32[4,16]{1,0:T(4,128)}, s32[4,16]{1,0:T(4,128)S(1)}, u32[]{:S(2)}) copy-start(s32[4,16]{1,0:T(4,128)S(1)} %collective-permute-done.8.refs_7_) | copy-start | bytes 772
  31.4 52.7 %collective-permute-start.9 = (bf16[16,32,128]{2,1,0:T(8,128)(2,1)S(1)}, bf16[16,32,128]{2,1,0:T(8,128)(2,1)S(1)}, u32[]{:S(2)}, u32[]{:S(2)}) collective-permute-start(bf16[16,32,128]{2,1,0:T(8,128)(2,1)S(1)} %get-tuple-element.298.refs_2_), channel_id=1, source_target_pairs={{0,3},{1,0},{2,1},{3,2},{4,7},{5,4},{6,5},{7,6},{8,11},{9,8},{10,9... | collective-permute-start | bytes 393224 | tf_op jit(solution)/shard_map/ppermute | solution.py:26
  31.4 2.4 %copy-start.6 = (s32[4,16]{1,0:T(4,128)}, s32[4,16]{1,0:T(4,128)S(1)}, u32[]{:S(2)}) copy-start(s32[4,16]{1,0:T(4,128)S(1)} %collective-permute-done.7.refs_6_) | copy-start | bytes 772
  31.4 52.7 %collective-permute-start.19 = (bf16[16,32,128]{2,1,0:T(8,128)(2,1)S(1)}, bf16[16,32,128]{2,1,0:T(8,128)(2,1)S(1)}, u32[]{:S(2)}, u32[]{:S(2)}) collective-permute-start(bf16[16,32,128]{2,1,0:T(8,128)(2,1)S(1)} %get-tuple-element.118), channel_id=1, source_target_pairs={{0,12},{4,0},{8,4},{12,8},{1,13},{5,1},{9,5},{13,9},{2,14},{6,2},{... | collective-permute-start | bytes 393224 | tf_op jit(solution)/shard_map/ppermute | solution.py:26
  33.7 1.8 %copy-start.7 = (s32[4,16]{1,0:T(4,128)}, s32[4,16]{1,0:T(4,128)S(1)}, u32[]{:S(2)}) copy-start(s32[4,16]{1,0:T(4,128)S(1)} %collective-permute-done.6.refs_5_) | copy-start | bytes 772
  33.7 50.4 %collective-permute-start.20 = (bf16[16,32,128]{2,1,0:T(8,128)(2,1)S(1)}, bf16[16,32,128]{2,1,0:T(8,128)(2,1)S(1)}, u32[]{:S(2)}, u32[]{:S(2)}) collective-permute-start(bf16[16,32,128]{2,1,0:T(8,128)(2,1)S(1)} %get-tuple-element.119), channel_id=1, source_target_pairs={{0,8},{4,12},{8,0},{12,4},{1,9},{5,13},{9,1},{13,5},{2,10},{6,14},... | collective-permute-start | bytes 393224 | tf_op jit(solution)/shard_map/ppermute | solution.py:26
  33.8 50.3 %collective-permute-start.21 = (bf16[16,32,128]{2,1,0:T(8,128)(2,1)S(1)}, bf16[16,32,128]{2,1,0:T(8,128)(2,1)S(1)}, u32[]{:S(2)}, u32[]{:S(2)}) collective-permute-start(bf16[16,32,128]{2,1,0:T(8,128)(2,1)S(1)} %get-tuple-element.120), channel_id=1, source_target_pairs={{0,4},{4,8},{8,12},{12,0},{1,5},{5,9},{9,13},{13,1},{2,6},{6,10},{... | collective-permute-start | bytes 393224 | tf_op jit(solution)/shard_map/ppermute | solution.py:26
  88.7 1.0 %copy-start.2 = (f32[16,4,4096]{2,1,0:T(4,128)}, f32[16,4,4096]{2,1,0:T(4,128)S(1)}, u32[]{:S(2)}) copy-start(f32[16,4,4096]{2,1,0:T(4,128)S(1)} %get-tuple-element.358) | copy-start | bytes 3145732

commit v2 on v1

v2 whole, which is shorter than its diff:
```python
import functools

import jax
import jax.numpy as jnp
from jax import lax
from jax.experimental import pallas as pl
from jax.experimental.pallas import tpu as pltpu
from jax.sharding import PartitionSpec as P

BS = 64
LANES = 128
ROWS = BS * BS // LANES
CAPACITY = 16
UNROLL = 4
SLOTS = 4
WORD = 16
TAIL = 16
FLAG = 16
CHOSEN = LANES - 1
IDLE = 63
VMEM = pltpu.VMEM
SMEM = pltpu.SMEM
BF16 = jnp.bfloat16
F32 = jnp.float32
I32 = jnp.int32


def shifted(block, axis, distance):
    size = lax.axis_size(axis)
    route = [(i, (i + distance) % size) for i in range(size)]
    return lax.ppermute(block, axis, route)


def words_of(rows, cols, row_count):
    return -(-rows * row_count // cols // WORD)


def describe_kernel(words, a_ref, b_ref, c_ref, out):
    count, slots = a_ref.shape[2], b_ref.shape[0]
    row_count = b_ref.shape[1]
    out[...] = jnp.zeros_like(out)
    out[0:2, 0:count] = a_ref[:, 0, :]
    columns = c_ref[...]
    bits = jnp.left_shift(1, columns % WORD)
    for w in range(words):
        here = jnp.where(columns // WORD == w, bits, 0)
        out[2 + w : 3 + w, 0:row_count] = jnp.sum(here, axis=0, keepdims=True)
    offered = b_ref[...]
    at = 2 + words
    out[at : at + slots, 0:row_count] = jnp.where(offered < 0, 31, offered % WORD)
    if words > 1:
        at = at + slots
        out[at : at + slots, 0:row_count] = jnp.where(offered < 0, 0, offered // WORD)


def describe(a_index, b_cols, c_cols, words):
    used = 2 + words + b_cols.shape[0] * (1 if words == 1 else 2)
    return pl.pallas_call(
        functools.partial(describe_kernel, words),
        out_shape=jax.ShapeDtypeStruct((-(-used // 8) * 8, LANES), I32),
        in_specs=[pl.BlockSpec(memory_space=VMEM)] * 3,
        out_specs=pl.BlockSpec(memory_space=VMEM),
        name="describe",
    )(a_index, b_cols, c_cols)


def is_kept(words, kept, row, offer, slot, k):
    bit = offer[2 + words + slot, k]
    if words == 1:
        word = kept[2, row]
    else:
        word = kept[2 + offer[2 + words + SLOTS + slot, k], row]
    return (word >> bit) & 1


def prepare_kernel(a_any, told, b_any, a_out, b_out, a_ref, b_ref, a_wide, b_wide, sems):
    copies = [
        pltpu.make_async_copy(a_any, a_ref, sems.at[0]),
        pltpu.make_async_copy(b_any, b_ref, sems.at[1]),
    ]
    for copy in copies:
        copy.start()
    source = lax.broadcasted_iota(I32, (LANES, LANES), 0)
    target = lax.broadcasted_iota(I32, (LANES, LANES), 1)
    wanted = (target // BS) * BS + 2 * (target % ROWS) + (target // ROWS) % 2
    order = (source == wanted).astype(BF16)
    copies[0].wait()
    slots = a_ref.shape[1]
    for t in range(ROWS):
        piece = a_ref[0, :, pl.ds(t * LANES, LANES)]
        a_wide[:, t, :] = jnp.dot(piece, order, preferred_element_type=F32)
    for s in range(slots):
        a_out[pl.ds(s * ROWS, ROWS), :] = a_wide[s].astype(BF16)
    indices = told[...].astype(F32)
    tail = jnp.concatenate([indices[:8], jnp.zeros((TAIL - 8, LANES), F32)], axis=0)
    a_out[pl.ds(slots * ROWS, TAIL), :] = tail.astype(BF16)
    copies[1].wait()
    row_count, slots = b_ref.shape[0], b_ref.shape[1]

    def one_row(k, carry):
        for t in range(ROWS):
            b_wide[pl.ds(t * slots, slots), :] = b_ref[k, :, pl.ds(t * LANES, LANES)].astype(F32)
        for n in range(slots):
            at = pl.multiple_of((k * slots + n) * ROWS, ROWS)
            b_out[pl.ds(at, ROWS), :] = b_wide[pl.ds(n, ROWS, stride=slots), :].astype(BF16)
        return carry

    lax.fori_loop(0, row_count, one_row, 0)


def prepare(a_blocks, told, b_blocks):
    slots = a_blocks.shape[1]
    blocks = b_blocks.shape[0] * b_blocks.shape[1]
    return pl.pallas_call(
        prepare_kernel,
        out_shape=(
            jax.ShapeDtypeStruct((slots * ROWS + TAIL, LANES), BF16),
            jax.ShapeDtypeStruct((blocks * ROWS, LANES), BF16),
        ),
        in_specs=[
            pl.BlockSpec(memory_space=pltpu.HBM),
            pl.BlockSpec(memory_space=VMEM),
            pl.BlockSpec(memory_space=pltpu.HBM),
        ],
        out_specs=(pl.BlockSpec(memory_space=VMEM),) * 2,
        scratch_shapes=[
            VMEM(a_blocks.shape, BF16),
            VMEM(b_blocks.shape, BF16),
            VMEM((slots, ROWS, LANES), F32),
            VMEM((b_blocks.shape[1] * ROWS, LANES), F32),
            pltpu.SemaphoreType.DMA((2,)),
        ],
        compiler_params=pltpu.CompilerParams(vmem_limit_bytes=24 << 20),
        cost_estimate=pl.CostEstimate(flops=1 << 24, bytes_accessed=16 << 20, transcendentals=0),
        name="prepare",
    )(a_blocks, told, b_blocks)


def fetch(copies, sems):
    started = [
        pltpu.make_async_copy(source, target, sems.at[at])
        for at, (source, target) in enumerate(copies)
    ]
    for copy in started:
        copy.start()
    for copy in started:
        copy.wait()


def pack_kernel(first, words, per_col, a_slots, *refs):
    refs = list(refs)
    base_ref = None if first else refs.pop(0)
    c_refs, a_refs, blocks, outs, most, c_s, a_s, chosen, seen, sems = refs
    peers = len(c_refs)
    row_count = blocks.shape[0] // ROWS // SLOTS
    fetch(
        [(ref, c_s.at[d]) for d, ref in enumerate(c_refs)]
        + [(ref, a_s.at[d]) for d, ref in enumerate(a_refs)],
        sems,
    )
    base = 0 if first else base_ref[0]
    grid_row = lax.axis_index("row")
    turn = grid_row % per_col * (peers // per_col) + lax.axis_index("col")

    def one_peer(d, top):
        place = (turn - grid_row + d + peers) % peers
        for k in range(row_count):
            seen[k] = 0
        count = jnp.int32(0)
        part = grid_row % per_col * a_slots if per_col > 1 else 0
        for s in range(a_slots):
            i = a_s[place, 0, part + s]
            k = jnp.maximum(a_s[place, 1, part + s], 0)
            live = (i >= 0).astype(I32)
            row = jnp.maximum(i, 0)
            before = seen[k]
            after = before
            for n in range(SLOTS):
                hit = is_kept(words, c_s.at[d], row, c_s.at[0], n, k) & live
                chosen[d, count] = k * SLOTS + n
                count = count + (hit & ~(before >> n))
                after = after | (hit << n)
            seen[k] = after
        chosen[d, CHOSEN] = count
        return jnp.maximum(top, count)

    top = lax.fori_loop(1, peers, one_peer, jnp.int32(0))
    most[0] = top
    sign = jnp.full((FLAG, LANES), top, I32).astype(F32).astype(BF16)
    for d in range(1, peers):
        out = outs[d - 1]
        count = chosen[d, CHOSEN]
        for x in range(CAPACITY):
            index = jnp.where(base + x < count, chosen[d, base + x], 0)
            block = blocks[pl.ds(pl.multiple_of(index * ROWS, ROWS), ROWS), :]
            out[pl.ds(x * ROWS, ROWS), :] = block
        out[pl.ds(CAPACITY * ROWS, FLAG), :] = sign


def pack(base, c_parts, a_parts, blocks, words, per_col, a_slots):
    peers = len(c_parts)
    first = base is None
    any_spec = pl.BlockSpec(memory_space=pl.ANY)
    smem_spec = pl.BlockSpec(memory_space=SMEM)
    vmem_spec = pl.BlockSpec(memory_space=VMEM)
    given = [] if first else [base]

    def kernel(*refs):
        refs = list(refs)
        base_refs = [] if first else [refs.pop(0)]
        grouped = [refs[:peers], refs[peers : 2 * peers], refs[2 * peers]]
        refs = refs[2 * peers + 1 :]
        grouped += [refs[: peers - 1]] + refs[peers - 1 :]
        pack_kernel(first, words, per_col, a_slots, *base_refs, *grouped)

    results = pl.pallas_call(
        kernel,
        out_shape=[jax.ShapeDtypeStruct((CAPACITY * ROWS + FLAG, LANES), BF16)] * (peers - 1)
        + [jax.ShapeDtypeStruct((1,), I32)],
        in_specs=[smem_spec] * len(given) + [any_spec] * (2 * peers) + [vmem_spec],
        out_specs=[vmem_spec] * (peers - 1) + [smem_spec],
        scratch_shapes=[
            SMEM((peers,) + c_parts[0].shape, I32),
            SMEM((peers,) + a_parts[0].shape, I32),
            SMEM((peers, LANES), I32),
            SMEM((blocks.shape[0] // ROWS // SLOTS,), I32),
            pltpu.SemaphoreType.DMA((2 * peers,)),
        ],
        compiler_params=pltpu.CompilerParams(vmem_limit_bytes=24 << 20),
        cost_estimate=pl.CostEstimate(flops=1 << 20, bytes_accessed=4 << 20, transcendentals=0),
        name="pack",
    )(*given, *c_parts, *a_parts, blocks)
    return results[:-1], results[-1]


def encode(a_slot, out, peer, place):
    return ((a_slot * 64 + out) * 64 + place) * 64 + peer


def list_kernel(words, span, per_col, a_slots, peers, *refs):
    a_all, b_refs = refs[0], refs[1 : 1 + peers]
    c_ref, items, total, a_s, a_v, a_i, b_s, c_s, spots, seen, places, sems = refs[1 + peers :]
    kept, row_count = c_ref.shape
    cols, a_rows = a_all.shape[0], a_all.shape[1]
    tails = [(a_all.at[h, pl.ds(a_rows - TAIL, TAIL)], a_v.at[h]) for h in range(cols)]
    fetch(
        tails + [(ref, b_s.at[d]) for d, ref in enumerate(b_refs)] + [(c_ref, c_s)],
        sems,
    )
    a_i[...] = a_v[:, 0:8, :].astype(F32).astype(I32)
    fetch([(a_i, a_s)], sems)
    grid_row = lax.axis_index("row")
    for i in range(row_count):
        for m in range(kept):
            spots[i * span + c_s[m, i]] = m

    def one_peer(d, length):
        group = (grid_row + d) % peers
        holder = group // per_col
        part = group % per_col * a_slots if per_col > 1 else 0
        own = d == 0
        for k in range(row_count):
            seen[k] = 0
        count = jnp.int32(0)
        for s in range(a_slots):
            i = a_s[holder, 0, part + s]
            k = jnp.maximum(a_s[holder, 1, part + s], 0)
            live = (i >= 0).astype(I32)
            row = jnp.maximum(i, 0)
            before = seen[k]
            after = before
            a_slot = holder * (per_col * a_slots) + part + s
            for n in range(SLOTS):
                hit = is_kept(words, b_s.at[0], row, b_s.at[d], n, k) & live
                column = b_s[d, 2 + words + n, k]
                if words > 1:
                    column = column + WORD * b_s[d, 2 + words + SLOTS + n, k]
                which = spots[row * span + jnp.where(hit == 1, column, 0)]
                fresh = hit & ~(before >> n)
                spot = k * SLOTS + n
                place = jnp.where(fresh == 1, count, places[spot])
                places[spot] = place
                stored = jnp.where(own, spot, place)
                items[length] = encode(a_slot, row * kept + which, d, stored)
                length = length + hit
                count = count + fresh
                after = after | (hit << n)
            seen[k] = after
        return length

    for spot in range(row_count * SLOTS):
        places[spot] = 0
    length = lax.fori_loop(0, peers, one_peer, jnp.int32(0))
    for u in range(UNROLL):
        items[length + u] = IDLE
    total[0] = length


def work_list(a_all, b_parts, c_cols, words, span, per_col, a_slots):
    cols, peers = a_all.shape[0], len(b_parts)
    row_count = c_cols.shape[1]
    most_items = peers * a_slots * SLOTS + UNROLL + SLOTS
    any_spec = pl.BlockSpec(memory_space=pl.ANY)
    smem_spec = pl.BlockSpec(memory_space=SMEM)
    return pl.pallas_call(
        functools.partial(list_kernel, words, span, per_col, a_slots, peers),
        out_shape=[
            jax.ShapeDtypeStruct((most_items,), I32),
            jax.ShapeDtypeStruct((1,), I32),
        ],
        in_specs=[any_spec] * (peers + 2),
        out_specs=[smem_spec] * 2,
        scratch_shapes=[
            SMEM((cols, 8, LANES), I32),
            VMEM((cols, TAIL, LANES), BF16),
            VMEM((cols, 8, LANES), I32),
            SMEM((peers,) + b_parts[0].shape, I32),
            SMEM(c_cols.shape, I32),
            SMEM((row_count * span,), I32),
            SMEM((row_count,), I32),
            SMEM((row_count * SLOTS,), I32),
            pltpu.SemaphoreType.DMA((cols + peers + 1,)),
        ],
        cost_estimate=pl.CostEstimate(flops=1 << 20, bytes_accessed=1 << 16, transcendentals=0),
        name="work_list",
    )(a_all, *b_parts, c_cols)


def multiply_kernel(first, peers, *refs):
    refs = list(refs)
    base_ref = previous = None
    if not first:
        base_ref, previous = refs.pop(0), refs.pop(0)
    items, total, most = refs.pop(0), refs.pop(0), refs.pop(0)
    a_all = refs.pop(0)
    own = refs.pop(0)
    b_refs = [refs.pop(0) for _ in range(peers - 1)]
    out, rounds, a_v, b_v, flags, sums, sems = refs
    own_rows = own.shape[0]
    held = (a_all.shape[1] - TAIL) // ROWS
    row_count, kept = out.shape[0], out.shape[1]
    copies = [(a_all, a_v)]
    copies += [(own, b_v.at[pl.ds(0, own_rows)])]
    width = CAPACITY * ROWS
    for d in range(peers - 1):
        copies += [
            (b_refs[d].at[pl.ds(0, width)], b_v.at[pl.ds(own_rows + d * width, width)]),
            (b_refs[d].at[pl.ds(width, FLAG)], flags.at[pl.ds(d * FLAG, FLAG)]),
        ]
    started = [
        pltpu.make_async_copy(source, target, sems.at[at])
        for at, (source, target) in enumerate(copies)
    ]
    for copy in started:
        copy.start()
    sums[...] = jnp.zeros_like(sums)
    for copy in started:
        copy.wait()
    base = 0 if first else base_ref[0]
    needed = jnp.maximum(most[0], jnp.max(flags[...].astype(F32)).astype(I32))
    rounds[0] = (needed + CAPACITY - 1) // CAPACITY
    low = lax.broadcasted_iota(I32, (ROWS, LANES), 1) < BS
    nothing = jnp.zeros((ROWS, LANES), BF16)

    def some_items(step, carry):
        for u in range(UNROLL):
            word = items[step * UNROLL + u]
            peer = word & 63
            place = (word >> 6) & 63
            target = (word >> 12) & 63
            a_slot = word >> 18
            inside = (place >= base) & (place < base + CAPACITY)
            own_item = peer == 0
            used = (inside & (peer > 0) & (peer < IDLE)) | (own_item if first else False)
            spot = jnp.where(
                own_item, place, own_rows // ROWS + (peer - 1) * CAPACITY + place - base
            )
            spot = jnp.where(used, spot, 0)
            inner = pl.multiple_of(a_slot % held * ROWS, ROWS)
            left = a_v[a_slot // held, pl.ds(inner, ROWS), :]
            block = b_v[pl.ds(pl.multiple_of(spot * ROWS, ROWS), ROWS), :]
            turned = jnp.concatenate([block[:, BS:], block[:, :BS]], axis=1)
            right = jnp.concatenate(
                [
                    jnp.where(low, block, nothing),
                    jnp.where(low, turned, nothing),
                    jnp.where(low, nothing, turned),
                    jnp.where(low, nothing, block),
                ],
                axis=0,
            )
            term = jnp.dot(left, right, preferred_element_type=F32)
            i = jnp.where(used, target // kept, row_count)
            m = target % kept
            sums[i, pl.ds(m, ROWS, stride=kept), :] += term
        return carry

    lax.fori_loop(0, (total[0] + UNROLL - 1) // UNROLL, some_items, 0)

    def one_row(i, carry):
        for t in range(ROWS):
            piece = sums[i, pl.ds(t * kept, kept), :]
            if previous is not None:
                piece = piece + previous[i, :, pl.ds(t * LANES, LANES)]
            out[i, :, pl.ds(t * LANES, LANES)] = piece
        return carry

    lax.fori_loop(0, row_count, one_row, 0)


def multiply(base, previous, items, total, most, a_all, own, b_parts, shape):
    first = base is None
    peers = len(b_parts) + 1
    any_spec = pl.BlockSpec(memory_space=pl.ANY)
    smem_spec = pl.BlockSpec(memory_space=SMEM)
    vmem_spec = pl.BlockSpec(memory_space=VMEM)
    given = [] if first else [base, previous]
    specs = [] if first else [smem_spec, vmem_spec]
    stored = own.shape[0] + (peers - 1) * CAPACITY * ROWS
    return pl.pallas_call(
        functools.partial(multiply_kernel, first, peers),
        out_shape=[jax.ShapeDtypeStruct(shape, F32), jax.ShapeDtypeStruct((1,), I32)],
        in_specs=specs + [smem_spec] * 3 + [any_spec] * (1 + peers),
        out_specs=[vmem_spec, smem_spec],
        scratch_shapes=[
            VMEM(a_all.shape, BF16),
            VMEM((stored, LANES), BF16),
            VMEM(((peers - 1) * FLAG, LANES), BF16),
            VMEM((shape[0] + 1, ROWS * shape[1], LANES), F32),
            pltpu.SemaphoreType.DMA((2 * peers,)),
        ],
        compiler_params=pltpu.CompilerParams(vmem_limit_bytes=32 << 20),
        cost_estimate=pl.CostEstimate(flops=1 << 26, bytes_accessed=4 << 20, transcendentals=0),
        name="multiply",
    )(*given, items, total, most, a_all, own, *b_parts)


def send_rows(parts):
    return [shifted(part, "row", -(d + 1)) for d, part in enumerate(parts)]


def index_parts(told, rows, cols, per_col):
    parts = []
    for d in range(rows):
        route = []
        for r in range(rows):
            for c in range(cols):
                turn = (r + d) % rows
                target = (c * per_col + turn // cols) * cols + turn % cols
                route.append((r * cols + c, target))
        parts.append(lax.ppermute(told, ("row", "col"), route))
    return parts


def shards(a_blocks, a_index, b_blocks, b_cols, c_cols):
    rows = lax.axis_size("row")
    cols = lax.axis_size("col")
    per_col = rows // cols
    a_slots = a_blocks.shape[1] // per_col
    row_count = b_blocks.shape[0]
    words = words_of(rows, cols, row_count)
    span = words * WORD
    c_turned = c_cols.T
    told = describe(a_index, b_cols.T, c_turned, words)
    a_near = index_parts(told, rows, cols, per_col)
    told_rows = [told] + [shifted(told, "row", d) for d in range(1, rows)]
    a_ready, own = prepare(a_blocks, told, b_blocks)
    a_all = lax.all_gather(a_ready, "col")

    packed, most = pack(None, told_rows, a_near, own, words, per_col, a_slots)
    arrived = send_rows(packed)
    ahead = [told_rows[(rows - d) % rows] for d in range(rows)]
    items, total = work_list(a_all, ahead, c_turned, words, span, per_col, a_slots)
    shape = (row_count, c_cols.shape[1], BS * BS)
    sums, rounds = multiply(None, None, items, total, most, a_all, own, arrived, shape)

    def more(state):
        return state[0] < rounds[0]

    def one_round(state):
        at, sums = state
        base = jnp.reshape(at * CAPACITY, (1,))
        packed, _ = pack(base, told_rows, a_near, own, words, per_col, a_slots)
        arrived = send_rows(packed)
        sums, _ = multiply(base, sums, items, total, most, a_all, own, arrived, shape)
        return at + 1, sums

    return lax.while_loop(more, one_round, (jnp.int32(1), sums))[1]


def solution(mesh):
    return jax.shard_map(
        shards,
        mesh=mesh,
        in_specs=(
            P(("sys", "row"), "col", None),
            P(None, ("sys", "row"), "col"),
            P(("sys", "row"), "col", None),
            P(("sys", "row"), "col"),
            P(("sys", "row"), "col"),
        ),
        out_specs=P(("sys", "row"), "col", None),
        check_vma=False,
    )
```

time: 89.9 us -> 46.4 us (0.52)
  blocking collectives: 41.3 us -> 9.07 us
  starting transfers between devices: 27.1 us -> 17.2 us
  waiting for transfers between devices: 2.06 us -> 0.03 us
  Pallas kernels: 15.4 us -> 16.3 us
    pmax x1 -> x0, blocking collectives: 41.3 us -> none  [shards(): lax.pmax(most[0], ('sys', 'row', 'col')) + CAPACITY - 1]
    all_gather x0 -> x1, blocking collectives: none -> 9.07 us  [shards(): a_all = lax.all_gather(a_ready, 'col')]
    ppermute x15 -> x6, starting transfers between devices: 18.2 us -> 10.8 us  [shifted(): return lax.ppermute(block, axis, route)]
    ppermute x4, starting transfers between devices: 8.96 us -> 6.33 us  [index_parts(): parts.append(lax.ppermute(told, ('row', 'col'), route))]
    ppermute x15 -> x6, waiting for transfers between devices: 2.05 us -> 0.02 us  [shifted(): return lax.ppermute(block, axis, route)]
    pallas_call x4 -> x5, Pallas kernels: 15.4 us -> 16.3 us  [the longest x1 6.38 us: work_list(): pl.pallas_call(functools.partial(list_kernel, words, span, per_col, a_slo...]
    unnamed x24 -> x6, local copies, waits for them, and re-layouts: 2.95 us -> 2.91 us
  transfers between devices with their start and end apart: 19 -> 10, of which waited for: 2 -> 0; matrix products, arithmetic and copies ran while one was open for 0% -> 0% of each run, Pallas kernels for 11% -> 16%
where the time goes in v2:
time: 46.4 us; the launch traced here: 46.2 us
  starting transfers between devices  17.2 us (37%)
  Pallas kernels  16.3 us (35%)
  blocking collectives  9.07 us (20%)
  local copies, waits for them, and re-layouts  2.91 us (6%)
  loops' own time  0.63 us (1%)
    ppermute x6, starting transfers between devices, shifted(): return lax.ppermute(block, axis, route)  10.8 us
    all_gather x1, blocking collectives, shards(): a_all = lax.all_gather(a_ready, 'col')  9.07 us
    pallas_call x1, Pallas kernels, work_list(): pl.pallas_call(functools.partial(list_kernel, words, span, per_col, a_slo...  6.38 us
    ppermute x4, starting transfers between devices, index_parts(): parts.append(lax.ppermute(told, ('row', 'col'), route))  6.33 us
    pallas_call x1, Pallas kernels, multiply(): pl.pallas_call(functools.partial(multiply_kernel, first, peers), out_shap...  4.95 us
    pallas_call x1, Pallas kernels, pack(): pl.pallas_call(kernel, out_shape=[jax.ShapeDtypeStruct((CAPACITY * ROWS +...  3.25 us
    unnamed x6, local copies, waits for them, and re-layouts  2.91 us
    pallas_call x1, Pallas kernels, prepare(): pl.pallas_call(prepare_kernel, out_shape=(jax.ShapeDtypeStruct((slots * R...  0.95 us
  transfers between devices with their start and end apart: 10, of which 0 were waited for; matrix products, arithmetic and copies ran while one was open for 0% of the time, Pallas kernels for 16%

profile of v2, /device:TPU:0, one launch (start us, length us, event | category | flops | bytes accessed | tf_op | source)
XLA Modules:
  0.0 46.2 jit_solution(6372818076349603863)
XLA Ops:
  0.0 0.7 %describe.1.told.refs_1_.refs_0_ = s32[8,128]{1,0:T(8,128)S(1)} custom-call(s32[2,1,16]{2,1,0:T(1,128)} %a_ref.1, s32[4,16]{1,0:T(4,128)} %bitcast.13, s32[4,16]{1,0:T(4,128)} %bitcast.11), custom_call_target="tpu_custom_call" | custom-call | tf_op jit(solution)/shard_map/describe/pallas_call | solution.py:58
  0.7 2.4 %collective-permute-start.9 = (s32[8,128]{1,0:T(8,128)S(1)}, s32[8,128]{1,0:T(8,128)S(1)}, u32[]{:S(2)}, u32[]{:S(2)}) collective-permute-start(s32[8,128]{1,0:T(8,128)S(1)} %describe.1.told.refs_1_.refs_0_), channel_id=1, source_target_pairs={{0,3},{1,7},{2,11},{3,15},{4,0},{5,4},{6,8},{7,12},{8,1},{9,5},{10... | collective-permute-start | bytes 12296 | tf_op jit(solution)/shard_map/ppermute | solution.py:451
  3.2 2.6 %collective-permute-start.8 = (s32[8,128]{1,0:T(8,128)S(1)}, s32[8,128]{1,0:T(8,128)S(1)}, u32[]{:S(2)}, u32[]{:S(2)}) collective-permute-start(s32[8,128]{1,0:T(8,128)S(1)} %describe.1.told.refs_1_.refs_0_), channel_id=1, source_target_pairs={{0,2},{1,6},{2,10},{3,14},{4,3},{5,7},{6,11},{7,15},{8,0},{9,4},{1... | collective-permute-start | bytes 12296 | tf_op jit(solution)/shard_map/ppermute | solution.py:451
  5.8 0.6 %collective-permute-start.7 = (s32[8,128]{1,0:T(8,128)S(1)}, s32[8,128]{1,0:T(8,128)S(1)}, u32[]{:S(2)}, u32[]{:S(2)}) collective-permute-start(s32[8,128]{1,0:T(8,128)S(1)} %describe.1.told.refs_1_.refs_0_), channel_id=1, source_target_pairs={{0,1},{1,5},{2,9},{3,13},{4,2},{5,6},{6,10},{7,14},{8,3},{9,7},{10... | collective-permute-start | bytes 12296 | tf_op jit(solution)/shard_map/ppermute | solution.py:451
  6.4 0.6 %collective-permute-start.6 = (s32[8,128]{1,0:T(8,128)S(1)}, s32[8,128]{1,0:T(8,128)S(1)}, u32[]{:S(2)}, u32[]{:S(2)}) collective-permute-start(s32[8,128]{1,0:T(8,128)S(1)} %describe.1.told.refs_1_.refs_0_), channel_id=1, source_target_pairs={{0,0},{1,4},{2,8},{3,12},{4,1},{5,5},{6,9},{7,13},{8,2},{9,6},{10,... | collective-permute-start | bytes 12296 | tf_op jit(solution)/shard_map/ppermute | solution.py:451
  7.1 3.9 %collective-permute-start.5 = (s32[8,128]{1,0:T(8,128)S(1)}, s32[8,128]{1,0:T(8,128)S(1)}, u32[]{:S(2)}, u32[]{:S(2)}) collective-permute-start(s32[8,128]{1,0:T(8,128)S(1)} %describe.1.told.refs_1_.refs_0_), channel_id=1, source_target_pairs={{0,4},{4,8},{8,12},{12,0},{1,5},{5,9},{9,13},{13,1},{2,6},{6,10},{... | collective-permute-start | bytes 12296 | tf_op jit(solution)/shard_map/ppermute | solution.py:31
  11.0 0.0 collective-permute-done.9.refs_7_
  11.0 2.8 %collective-permute-start.4 = (s32[8,128]{1,0:T(8,128)S(1)}, s32[8,128]{1,0:T(8,128)S(1)}, u32[]{:S(2)}, u32[]{:S(2)}) collective-permute-start(s32[8,128]{1,0:T(8,128)S(1)} %describe.1.told.refs_1_.refs_0_), channel_id=1, source_target_pairs={{0,8},{4,12},{8,0},{12,4},{1,9},{5,13},{9,1},{13,5},{2,10},{6,14},... | collective-permute-start | bytes 12296 | tf_op jit(solution)/shard_map/ppermute | solution.py:31
  13.8 0.0 collective-permute-done.8.refs_6_
  13.8 1.0 %collective-permute-start.3 = (s32[8,128]{1,0:T(8,128)S(1)}, s32[8,128]{1,0:T(8,128)S(1)}, u32[]{:S(2)}, u32[]{:S(2)}) collective-permute-start(s32[8,128]{1,0:T(8,128)S(1)} %describe.1.told.refs_1_.refs_0_), channel_id=1, source_target_pairs={{0,12},{4,0},{8,4},{12,8},{1,13},{5,1},{9,5},{13,9},{2,14},{6,2},{... | collective-permute-start | bytes 12296 | tf_op jit(solution)/shard_map/ppermute | solution.py:31
  14.8 0.0 copy-start
  14.8 1.0 %copy-done = bf16[16,4,4096]{2,1,0:T(4,128)(2,1)S(1)} copy-done((bf16[16,4,4096]{2,1,0:T(4,128)(2,1)S(1)}, bf16[16,4,4096]{2,1,0:T(4,128)(2,1)}, u32[]{:S(2)}) %copy-start) | copy-done | bytes 524312
  15.8 0.9 %copy-done.1 = bf16[1,16,4096]{2,1,0:T(8,128)(2,1)S(1)} copy-done((bf16[1,16,4096]{2,1,0:T(8,128)(2,1)S(1)}, bf16[1,16,4096]{2,1,0:T(8,128)(2,1)}, u32[]{:S(2)}) %copy-start.1) | copy-done | bytes 131096
  16.7 0.9 %prepare.1 = (bf16[528,128]{1,0:T(8,128)(2,1)S(1)}, bf16[2048,128]{1,0:T(8,128)(2,1)S(1)}) custom-call(bf16[1,16,4096]{2,1,0:T(8,128)(2,1)S(1)} %copy-done.1, s32[8,128]{1,0:T(8,128)S(1)} %describe.1.told.refs_1_.refs_0_, bf16[16,4,4096]{2,1,0:T(4,128)(2,1)S(1)} %copy-done), custom_call_target="tpu_custom_call" | custom-call | flops 16777216 | bytes 16777216 | tf_op jit(solution)/shard_map/prepare/pallas_call | solution.py:114
  17.7 0.0 collective-permute-done.7.refs_5_
  17.7 0.0 collective-permute-done.6.refs_4_
  17.7 0.0 collective-permute-done.5.refs_4_.refs_1_
  17.7 0.0 collective-permute-done.4.refs_3_.refs_2_
  17.7 0.0 collective-permute-done.3.refs_2_.refs_3_
  17.7 3.2 %pack.2 = (bf16[528,128]{1,0:T(8,128)(2,1)S(1)}, bf16[528,128]{1,0:T(8,128)(2,1)S(1)}, bf16[528,128]{1,0:T(8,128)(2,1)S(1)}, s32[1]{0:T(128)}) custom-call(s32[8,128]{1,0:T(8,128)S(1)} %describe.1.told.refs_1_.refs_0_, s32[8,128]{1,0:T(8,128)S(1)} %collective-permute-done.5.refs_4_.refs_1_, s32[8,128]{1,0:T(8,128)S(1)} %collective-permute-done.4.refs_3_.refs_2_, ...), custom_call_target="tpu_custom_call" | custom-call | flops 1048576 | bytes 4194304 | tf_op jit(solution)/shard_map/pack/pallas_call | solution.py:216
  21.0 2.5 %collective-permute-start.10 = (bf16[528,128]{1,0:T(8,128)(2,1)S(1)}, bf16[528,128]{1,0:T(8,128)(2,1)S(1)}, u32[]{:S(2)}, u32[]{:S(2)}) collective-permute-start(bf16[528,128]{1,0:T(8,128)(2,1)S(1)} %get-tuple-element.107), channel_id=1, source_target_pairs={{0,12},{4,0},{8,4},{12,8},{1,13},{5,1},{9,5},{13,9},{2,14},{6,2},{... | collective-permute-start | bytes 405512 | tf_op jit(solution)/shard_map/ppermute | solution.py:31
  23.5 0.1 collective-permute-start.11
  23.6 0.6 %collective-permute-start.12 = (bf16[528,128]{1,0:T(8,128)(2,1)S(1)}, bf16[528,128]{1,0:T(8,128)(2,1)S(1)}, u32[]{:S(2)}, u32[]{:S(2)}) collective-permute-start(bf16[528,128]{1,0:T(8,128)(2,1)S(1)} %get-tuple-element.109), channel_id=1, source_target_pairs={{0,4},{4,8},{8,12},{12,0},{1,5},{5,9},{9,13},{13,1},{2,6},{6,10},{... | collective-permute-start | bytes 405512 | tf_op jit(solution)/shard_map/ppermute | solution.py:31
  24.1 9.1 %all-gather = bf16[2112,128]{1,0:T(8,128)(2,1)S(1)} all-gather(bf16[528,128]{1,0:T(8,128)(2,1)S(1)} %get-tuple-element.102), channel_id=2, replica_groups=mesh['sys'=2,'row'=4,'col'=4] {'col'}, dimensions={0}, use_global_device_ids=true | all-gather | bytes 675840 | tf_op jit(solution)/shard_map/all_gather | solution.py:468
  33.2 6.4 %work_list.1 = (s32[264]{0:T(512)S(1)}, s32[1]{0:T(128)}) custom-call(bf16[4,528,128]{2,1,0:T(8,128)(2,1)S(1)} %bitcast.8, s32[8,128]{1,0:T(8,128)S(1)} %describe.1.told.refs_1_.refs_0_, s32[8,128]{1,0:T(8,128)S(1)} %collective-permute-done.3.refs_2_.refs_3_, s32[8,128]{1,0:T(8,128)S(1)} %collective-permute-done.4.refs_3_.refs_2_, ...), custom_call_target="tpu_custom_call" | custom-call | flops 1048576 | bytes 65536 | tf_op jit(solution)/shard_map/work_list/pallas_call | solution.py:305
  39.6 0.0 collective-permute-done.10.refs_5_
  39.6 0.0 collective-permute-done.11.refs_6_
  39.6 0.0 collective-permute-done.12.refs_7_
  39.6 5.0 %multiply.2 = (f32[16,4,4096]{2,1,0:T(4,128)S(1)}, s32[1]{0:T(128)}) custom-call(s32[264]{0:T(512)S(1)} %get-tuple-element.263.refs_0_, s32[1]{0:T(128)} %get-tuple-element.264.refs_1_, s32[1]{0:T(128)} %get-tuple-element.265.refs_2_, bf16[4,528,128]{2,1,0:T(8,128)(2,1)S(1)} %bitcast.9, bf16[2048,128]{1,0:T(8,128)(2,1)S(1)} %get-tuple-element.262.refs_8_.refs_4_, ...), custom_call_target="tpu_custom_call" | custom-call | flops 67108864 | bytes 4194304 | tf_op jit(solution)/shard_map/multiply/pallas_call | solution.py:420
  44.6 0.6 %while.10 = (s32[]{:T(128)}, f32[16,4,4096]{2,1,0:T(4,128)S(1)}, s32[1]{0:T(128)}, s32[8,128]{1,0:T(8,128)S(1)}, s32[8,128]{1,0:T(8,128)S(1)}, /*index=5*/s32[8,...) while((s32[]{:T(128)}, f32[16,4,4096]{2,1,0:T(4,128)S(1)}, ...), condition=%wide.region_1.0_spmd, body=%wide.region_0.0_spmd.sunk | while | flops 68157440 | bytes 12108073 | solution.py:488
  45.2 0.0 copy-start.2
  45.2 1.0 %copy-done.2 = f32[16,4,4096]{2,1,0:T(4,128)} copy-done((f32[16,4,4096]{2,1,0:T(4,128)}, f32[16,4,4096]{2,1,0:T(4,128)S(1)}, u32[]{:S(2)}) %copy-start.2) | copy-done | bytes 1048600
  (1 shorter events, 0.0 us)
Async XLA Ops:
  0.7 10.3 %collective-permute-start.9 = (s32[8,128]{1,0:T(8,128)S(1)}, s32[8,128]{1,0:T(8,128)S(1)}, u32[]{:S(2)}, u32[]{:S(2)}) collective-permute-start(s32[8,128]{1,0:T(8,128)S(1)} %describe.1.told.refs_1_.refs_0_), channel_id=1, source_target_pairs={{0,3},{1,7},{2,11},{3,15},{4,0},{5,4},{6,8},{7,12},{8,1},{9,5},{10... | collective-permute-start | bytes 12296 | tf_op jit(solution)/shard_map/ppermute | solution.py:451
  3.2 10.6 %collective-permute-start.8 = (s32[8,128]{1,0:T(8,128)S(1)}, s32[8,128]{1,0:T(8,128)S(1)}, u32[]{:S(2)}, u32[]{:S(2)}) collective-permute-start(s32[8,128]{1,0:T(8,128)S(1)} %describe.1.told.refs_1_.refs_0_), channel_id=1, source_target_pairs={{0,2},{1,6},{2,10},{3,14},{4,3},{5,7},{6,11},{7,15},{8,0},{9,4},{1... | collective-permute-start | bytes 12296 | tf_op jit(solution)/shard_map/ppermute | solution.py:451
  5.8 11.9 %collective-permute-start.7 = (s32[8,128]{1,0:T(8,128)S(1)}, s32[8,128]{1,0:T(8,128)S(1)}, u32[]{:S(2)}, u32[]{:S(2)}) collective-permute-start(s32[8,128]{1,0:T(8,128)S(1)} %describe.1.told.refs_1_.refs_0_), channel_id=1, source_target_pairs={{0,1},{1,5},{2,9},{3,13},{4,2},{5,6},{6,10},{7,14},{8,3},{9,7},{10... | collective-permute-start | bytes 12296 | tf_op jit(solution)/shard_map/ppermute | solution.py:451
  6.4 11.3 %collective-permute-start.6 = (s32[8,128]{1,0:T(8,128)S(1)}, s32[8,128]{1,0:T(8,128)S(1)}, u32[]{:S(2)}, u32[]{:S(2)}) collective-permute-start(s32[8,128]{1,0:T(8,128)S(1)} %describe.1.told.refs_1_.refs_0_), channel_id=1, source_target_pairs={{0,0},{1,4},{2,8},{3,12},{4,1},{5,5},{6,9},{7,13},{8,2},{9,6},{10,... | collective-permute-start | bytes 12296 | tf_op jit(solution)/shard_map/ppermute | solution.py:451
  7.1 10.6 %collective-permute-start.5 = (s32[8,128]{1,0:T(8,128)S(1)}, s32[8,128]{1,0:T(8,128)S(1)}, u32[]{:S(2)}, u32[]{:S(2)}) collective-permute-start(s32[8,128]{1,0:T(8,128)S(1)} %describe.1.told.refs_1_.refs_0_), channel_id=1, source_target_pairs={{0,4},{4,8},{8,12},{12,0},{1,5},{5,9},{9,13},{13,1},{2,6},{6,10},{... | collective-permute-start | bytes 12296 | tf_op jit(solution)/shard_map/ppermute | solution.py:31
  11.0 6.7 %collective-permute-start.4 = (s32[8,128]{1,0:T(8,128)S(1)}, s32[8,128]{1,0:T(8,128)S(1)}, u32[]{:S(2)}, u32[]{:S(2)}) collective-permute-start(s32[8,128]{1,0:T(8,128)S(1)} %describe.1.told.refs_1_.refs_0_), channel_id=1, source_target_pairs={{0,8},{4,12},{8,0},{12,4},{1,9},{5,13},{9,1},{13,5},{2,10},{6,14},... | collective-permute-start | bytes 12296 | tf_op jit(solution)/shard_map/ppermute | solution.py:31
  13.8 3.9 %collective-permute-start.3 = (s32[8,128]{1,0:T(8,128)S(1)}, s32[8,128]{1,0:T(8,128)S(1)}, u32[]{:S(2)}, u32[]{:S(2)}) collective-permute-start(s32[8,128]{1,0:T(8,128)S(1)} %describe.1.told.refs_1_.refs_0_), channel_id=1, source_target_pairs={{0,12},{4,0},{8,4},{12,8},{1,13},{5,1},{9,5},{13,9},{2,14},{6,2},{... | collective-permute-start | bytes 12296 | tf_op jit(solution)/shard_map/ppermute | solution.py:31
  14.8 1.0 %copy-start = (bf16[16,4,4096]{2,1,0:T(4,128)(2,1)S(1)}, bf16[16,4,4096]{2,1,0:T(4,128)(2,1)}, u32[]{:S(2)}) copy-start(bf16[16,4,4096]{2,1,0:T(4,128)(2,1)} %b_any.1) | copy-start | bytes 1572868
  15.8 0.9 %copy-start.1 = (bf16[1,16,4096]{2,1,0:T(8,128)(2,1)S(1)}, bf16[1,16,4096]{2,1,0:T(8,128)(2,1)}, u32[]{:S(2)}) copy-start(bf16[1,16,4096]{2,1,0:T(8,128)(2,1)} %a_any.1) | copy-start | bytes 393220
  21.0 18.6 %collective-permute-start.10 = (bf16[528,128]{1,0:T(8,128)(2,1)S(1)}, bf16[528,128]{1,0:T(8,128)(2,1)S(1)}, u32[]{:S(2)}, u32[]{:S(2)}) collective-permute-start(bf16[528,128]{1,0:T(8,128)(2,1)S(1)} %get-tuple-element.107), channel_id=1, source_target_pairs={{0,12},{4,0},{8,4},{12,8},{1,13},{5,1},{9,5},{13,9},{2,14},{6,2},{... | collective-permute-start | bytes 405512 | tf_op jit(solution)/shard_map/ppermute | solution.py:31
  23.5 16.1 %collective-permute-start.11 = (bf16[528,128]{1,0:T(8,128)(2,1)S(1)}, bf16[528,128]{1,0:T(8,128)(2,1)S(1)}, u32[]{:S(2)}, u32[]{:S(2)}) collective-permute-start(bf16[528,128]{1,0:T(8,128)(2,1)S(1)} %get-tuple-element.108), channel_id=1, source_target_pairs={{0,8},{4,12},{8,0},{12,4},{1,9},{5,13},{9,1},{13,5},{2,10},{6,14},... | collective-permute-start | bytes 405512 | tf_op jit(solution)/shard_map/ppermute | solution.py:31
  23.6 16.0 %collective-permute-start.12 = (bf16[528,128]{1,0:T(8,128)(2,1)S(1)}, bf16[528,128]{1,0:T(8,128)(2,1)S(1)}, u32[]{:S(2)}, u32[]{:S(2)}) collective-permute-start(bf16[528,128]{1,0:T(8,128)(2,1)S(1)} %get-tuple-element.109), channel_id=1, source_target_pairs={{0,4},{4,8},{8,12},{12,0},{1,5},{5,9},{9,13},{13,1},{2,6},{6,10},{... | collective-permute-start | bytes 405512 | tf_op jit(solution)/shard_map/ppermute | solution.py:31
  45.2 1.0 %copy-start.2 = (f32[16,4,4096]{2,1,0:T(4,128)}, f32[16,4,4096]{2,1,0:T(4,128)S(1)}, u32[]{:S(2)}) copy-start(f32[16,4,4096]{2,1,0:T(4,128)S(1)} %get-tuple-element.317) | copy-start | bytes 3145732

commit v3 on v2

v3 whole, which is shorter than its diff:
```python
import functools

import jax
import jax.numpy as jnp
from jax import lax
from jax.experimental import pallas as pl
from jax.experimental.pallas import tpu as pltpu
from jax.sharding import PartitionSpec as P

BS = 64
LANES = 128
ROWS = BS * BS // LANES
CAPACITY = 16
UNROLL = 4
SLOTS = 4
WORD = 16
FLAG = 16
IDLE = 63
VMEM = pltpu.VMEM
SMEM = pltpu.SMEM
BF16 = jnp.bfloat16
F32 = jnp.float32
I32 = jnp.int32


def shifted(block, axis, distance):
    size = lax.axis_size(axis)
    route = [(i, (i + distance) % size) for i in range(size)]
    return lax.ppermute(block, axis, route)


A_ROW, A_COLUMN, RETAINED = 0, 1, 2
OFFERED = RETAINED + SLOTS
TOLD = 8


def describe_kernel(a_ref, b_ref, c_ref, out):
    count, row_count = a_ref.shape[2], b_ref.shape[1]
    out[...] = jnp.full(out.shape, -1, I32)
    out[0:2, 0:count] = a_ref[:, 0, :]
    out[RETAINED : RETAINED + c_ref.shape[0], 0:row_count] = c_ref[...]
    for n in range(b_ref.shape[0]):
        at = n * row_count
        out[OFFERED : OFFERED + 1, at : at + row_count] = b_ref[n : n + 1, :]


def describe(a_index, b_cols, c_cols):
    return pl.pallas_call(
        describe_kernel,
        out_shape=jax.ShapeDtypeStruct((TOLD, LANES), I32),
        in_specs=[pl.BlockSpec(memory_space=VMEM)] * 3,
        out_specs=pl.BlockSpec(memory_space=VMEM),
        name="describe",
    )(a_index, b_cols, c_cols)


def iota(shape, axis):
    return lax.broadcasted_iota(I32, shape, axis)


def along_lanes(left, right):
    return lax.dot_general(
        left.astype(BF16), right.astype(BF16), (((1,), (1,)), ((), ())), preferred_element_type=F32
    )


def demand(retained, offered, a_rows, a_columns, row_count, first_slot, a_slots):
    shape = (row_count, LANES)
    turned = along_lanes((iota(shape, 0) == iota(shape, 1)).astype(F32), retained.astype(F32))
    wanted = offered.astype(F32)
    kept = turned[:, 0:1] == wanted
    for m in range(1, SLOTS):
        kept = kept | (turned[:, m : m + 1] == wanted)
    lane = iota(shape, 1)
    mine = (lane >= first_slot) & (lane < first_slot + a_slots)
    by_row = ((iota(shape, 0) == a_rows) & mine).astype(F32)
    by_column = (iota((LANES, LANES), 0) % row_count == a_columns).astype(F32)
    uses = along_lanes(by_row, by_column)
    return jnp.max(jnp.where(kept & (uses > 0.5), 1.0, 0.0), axis=0, keepdims=True)


def layout_kernel(a_ref, b_ref, a_out, b_out, a_wide, b_wide):
    source = iota((LANES, LANES), 0)
    target = iota((LANES, LANES), 1)
    wanted = (target // BS) * BS + 2 * (target % ROWS) + (target // ROWS) % 2
    order = (source == wanted).astype(BF16)
    slots = a_ref.shape[1]
    for t in range(ROWS):
        piece = a_ref[0, :, pl.ds(t * LANES, LANES)]
        a_wide[:, t, :] = jnp.dot(piece, order, preferred_element_type=F32)
    for s in range(slots):
        a_out[pl.ds(s * ROWS, ROWS), :] = a_wide[s].astype(BF16)
    row_count, slots = b_ref.shape[0], b_ref.shape[1]

    def one_row(k, carry):
        for t in range(ROWS):
            b_wide[pl.ds(t * slots, slots), :] = b_ref[k, :, pl.ds(t * LANES, LANES)].astype(F32)
        for n in range(slots):
            at = pl.multiple_of((n * row_count + k) * ROWS, ROWS)
            b_out[pl.ds(at, ROWS), :] = b_wide[pl.ds(n, ROWS, stride=slots), :].astype(BF16)
        return carry

    lax.fori_loop(0, row_count, one_row, 0)


def layout(a_blocks, b_blocks):
    slots = a_blocks.shape[1]
    blocks = b_blocks.shape[0] * b_blocks.shape[1]
    return pl.pallas_call(
        layout_kernel,
        out_shape=(
            jax.ShapeDtypeStruct((slots * ROWS, LANES), BF16),
            jax.ShapeDtypeStruct((blocks * ROWS, LANES), BF16),
        ),
        in_specs=[pl.BlockSpec(memory_space=VMEM)] * 2,
        out_specs=(pl.BlockSpec(memory_space=VMEM),) * 2,
        scratch_shapes=[
            VMEM((slots, ROWS, LANES), F32),
            VMEM((b_blocks.shape[1] * ROWS, LANES), F32),
        ],
        compiler_params=pltpu.CompilerParams(vmem_limit_bytes=24 << 20),
        cost_estimate=pl.CostEstimate(flops=1 << 24, bytes_accessed=4 << 20, transcendentals=0),
        name="layout",
    )(a_blocks, b_blocks)


def fetch(copies, sems):
    started = [
        pltpu.make_async_copy(source, target, sems.at[at])
        for at, (source, target) in enumerate(copies)
    ]
    for copy in started:
        copy.start()
    for copy in started:
        copy.wait()


def pack_kernel(first, peers, per_col, a_slots, *refs):
    refs = list(refs)
    base = 0 if first else refs.pop(0)[0]
    told, b_ref = refs.pop(0), refs.pop(0)
    outs = refs[: peers - 1]
    most, picks, wide, packed = refs[peers - 1 :]
    row_count, slots = b_ref.shape[0], b_ref.shape[1]
    blocks = row_count * slots
    cols = told.shape[0] // peers
    grid_row = lax.axis_index("row")
    grid_col = lax.axis_index("col")
    offered = told[grid_row * cols + grid_col, pl.ds(OFFERED, 1), :]
    before = (iota((LANES, LANES), 0) < iota((LANES, LANES), 1)).astype(BF16)

    def one_peer(d, top):
        row = (grid_row + peers - d) % peers
        retained = told[row * cols + grid_col, pl.ds(RETAINED, SLOTS), :]
        a_from = row * cols + grid_row // per_col
        a_rows, a_columns = told[a_from, pl.ds(A_ROW, 1), :], told[a_from, pl.ds(A_COLUMN, 1), :]
        needed = demand(
            retained, offered, a_rows, a_columns, row_count, grid_row % per_col * a_slots, a_slots
        )
        many = jnp.broadcast_to(needed, (8, LANES)).astype(BF16)
        place = jnp.dot(many, before, preferred_element_type=F32)[0:1]
        place = jnp.where(needed > 0.5, place, -1.0).astype(I32)
        pick = (place == iota((CAPACITY, LANES), 0) + base).astype(BF16)
        picks[pl.ds(pl.multiple_of((d - 1) * CAPACITY, CAPACITY), CAPACITY), :] = pick
        return jnp.maximum(top, jnp.sum(needed, axis=1, keepdims=True))

    if peers <= 8:
        top = jnp.zeros((1, 1), F32)
        for d in range(1, peers):
            top = one_peer(d, top)
    else:
        top = lax.fori_loop(1, peers, one_peer, jnp.zeros((1, 1), F32))
    most[...] = jnp.broadcast_to(top, most.shape)
    wide[...] = b_ref[...].astype(F32)
    pick = picks[...][:, :blocks]
    for t in range(ROWS):
        lanes = pl.ds(t * LANES, LANES)
        flat = jnp.concatenate([wide[:, n, lanes] for n in range(slots)], axis=0).astype(BF16)
        packed[:, t, :] = jnp.dot(pick, flat, preferred_element_type=F32)
    for d in range(1, peers):
        out = outs[d - 1]
        for x in range(CAPACITY):
            out[pl.ds(x * ROWS, ROWS), :] = packed[(d - 1) * CAPACITY + x].astype(BF16)
        out[pl.ds(CAPACITY * ROWS, FLAG), :] = jnp.broadcast_to(top, (FLAG, LANES)).astype(BF16)


def pack(base, told_all, b_blocks, peers, per_col, a_slots):
    first = base is None
    smem_spec = pl.BlockSpec(memory_space=SMEM)
    vmem_spec = pl.BlockSpec(memory_space=VMEM)
    given = [] if first else [base]
    results = pl.pallas_call(
        functools.partial(pack_kernel, first, peers, per_col, a_slots),
        out_shape=[jax.ShapeDtypeStruct((CAPACITY * ROWS + FLAG, LANES), BF16)] * (peers - 1)
        + [jax.ShapeDtypeStruct((8, LANES), F32)],
        in_specs=[smem_spec] * len(given) + [vmem_spec] * 2,
        out_specs=[vmem_spec] * peers,
        scratch_shapes=[
            VMEM(((peers - 1) * CAPACITY, LANES), BF16),
            VMEM(b_blocks.shape, F32),
            VMEM(((peers - 1) * CAPACITY, ROWS, LANES), F32),
        ],
        compiler_params=pltpu.CompilerParams(vmem_limit_bytes=32 << 20),
        cost_estimate=pl.CostEstimate(flops=1 << 20, bytes_accessed=4 << 20, transcendentals=0),
        name="pack",
    )(*given, told_all, b_blocks)
    return results[:-1], results[-1]


def encode(a_slot, out, peer, place):
    return ((a_slot * 64 + out) * 64 + place) * 64 + peer


def list_kernel(span, per_col, a_slots, peers, told, items, total, *scratch):
    a_s, b_s, c_s, spots, bits, seen, places, sems = scratch
    cols = told.shape[0] // peers
    row_count = seen.shape[0]
    grid_row = lax.axis_index("row")
    grid_col = lax.axis_index("col")
    own = grid_row * cols + grid_col
    copies = [(told.at[own], c_s)]
    copies += [(told.at[grid_row * cols + h], a_s.at[h]) for h in range(cols)]
    copies += [(told.at[g * cols + grid_col], b_s.at[g]) for g in range(peers)]
    fetch(copies, sems)
    words = span // WORD
    for i in range(row_count):
        columns = [c_s[RETAINED + m, i] for m in range(SLOTS)]
        for w in range(words):
            held = [jnp.left_shift(1, c % WORD) for c in columns]
            if words > 1:
                held = [jnp.where(c // WORD == w, h, 0) for c, h in zip(columns, held)]
            bits[i * words + w] = functools.reduce(jnp.bitwise_or, held)
        for m, c in enumerate(columns):
            spots[i * span + c] = m

    def one_peer(d, length):
        group = (grid_row + d) % peers
        holder = group // per_col
        part = group % per_col * a_slots if per_col > 1 else 0
        for spot in range(row_count * SLOTS):
            seen_row = spot % row_count
            if spot < row_count:
                seen[seen_row] = 0
        for s in range(a_slots):
            i = a_s[holder, A_ROW, part + s]
            k = jnp.maximum(a_s[holder, A_COLUMN, part + s], 0)
            live = (i >= 0).astype(I32)
            row = jnp.maximum(i, 0)
            after = seen[k]
            for n in range(SLOTS):
                column = b_s[group, OFFERED, n * row_count + k]
                safe = jnp.maximum(column, 0)
                word = bits[row * words + (safe // WORD if words > 1 else 0)]
                hit = (word >> (safe % WORD)) & live & (column >= 0).astype(I32)
                after = after | (hit << n)
                which = spots[row * span + jnp.where(hit == 1, safe, c_s[RETAINED, row])]
                items[length] = encode(
                    holder * per_col * a_slots + part + s,
                    row * SLOTS + which,
                    d,
                    n * row_count + k,
                )
                length = length + hit
            seen[k] = after
        count = jnp.int32(0)
        for n in range(SLOTS):
            for k in range(row_count):
                spot = n * row_count + k
                places[d, spot] = jnp.where(d == 0, spot, count)
                count = count + ((seen[k] >> n) & 1)
        return length

    length = lax.fori_loop(0, peers, one_peer, jnp.int32(0))
    for u in range(UNROLL):
        items[length + u] = IDLE
    total[0] = length

    def settle(y, carry):
        word = items[y]
        peer, spot = word & 63, (word >> 6) & 63
        items[y] = word + ((places[peer, spot] - spot) << 6)
        return carry

    lax.fori_loop(0, length, settle, 0)


def work_list(told_all, peers, row_count, span, per_col, a_slots):
    cols = told_all.shape[0] // peers
    most_items = peers * a_slots * SLOTS + UNROLL + SLOTS
    return pl.pallas_call(
        functools.partial(list_kernel, span, per_col, a_slots, peers),
        out_shape=[
            jax.ShapeDtypeStruct((most_items,), I32),
            jax.ShapeDtypeStruct((1,), I32),
        ],
        in_specs=[pl.BlockSpec(memory_space=pl.ANY)],
        out_specs=[pl.BlockSpec(memory_space=SMEM)] * 2,
        scratch_shapes=[
            SMEM((cols, TOLD, LANES), I32),
            SMEM((peers, TOLD, LANES), I32),
            SMEM((TOLD, LANES), I32),
            SMEM((row_count * span,), I32),
            SMEM((row_count * (span // WORD),), I32),
            SMEM((row_count,), I32),
            SMEM((peers, LANES), I32),
            pltpu.SemaphoreType.DMA((cols + peers + 1,)),
        ],
        cost_estimate=pl.CostEstimate(flops=1 << 20, bytes_accessed=1 << 16, transcendentals=0),
        name="work_list",
    )(told_all)


def multiply_kernel(first, peers, cols, *refs):
    refs = list(refs)
    base_ref = previous = None
    if not first:
        base_ref, previous = refs.pop(0), refs.pop(0)
    items, total, most = refs.pop(0), refs.pop(0), refs.pop(0)
    a_refs = [refs.pop(0) for _ in range(cols)]
    own = refs.pop(0)
    b_refs = [refs.pop(0) for _ in range(peers - 1)]
    out, rounds, a_v, b_v, flags, sums, sems = refs
    own_rows = own.shape[0]
    held = a_refs[0].shape[0] // ROWS
    grid_col = lax.axis_index("col")
    row_count, kept = out.shape[0], out.shape[1]
    copies = [(ref, a_v.at[(grid_col + h) % cols]) for h, ref in enumerate(a_refs)]
    copies += [(own, b_v.at[pl.ds(0, own_rows)])]
    width = CAPACITY * ROWS
    for d in range(peers - 1):
        copies += [
            (b_refs[d].at[pl.ds(0, width)], b_v.at[pl.ds(own_rows + d * width, width)]),
            (b_refs[d].at[pl.ds(width, FLAG)], flags.at[pl.ds(d * FLAG, FLAG)]),
        ]
    started = [
        pltpu.make_async_copy(source, target, sems.at[at])
        for at, (source, target) in enumerate(copies)
    ]
    for copy in started:
        copy.start()
    sums[...] = jnp.zeros_like(sums)
    for copy in started:
        copy.wait()
    base = 0 if first else base_ref[0]
    needed = jnp.maximum(jnp.max(most[...]), jnp.max(flags[...].astype(F32))).astype(I32)
    rounds[0] = (needed + CAPACITY - 1) // CAPACITY
    low = lax.broadcasted_iota(I32, (ROWS, LANES), 1) < BS
    nothing = jnp.zeros((ROWS, LANES), BF16)

    def some_items(step, carry):
        for u in range(UNROLL):
            word = items[step * UNROLL + u]
            peer = word & 63
            place = (word >> 6) & 63
            target = (word >> 12) & 63
            a_slot = word >> 18
            inside = (place >= base) & (place < base + CAPACITY)
            own_item = peer == 0
            used = (inside & (peer > 0) & (peer < IDLE)) | (own_item if first else False)
            spot = jnp.where(
                own_item, place, own_rows // ROWS + (peer - 1) * CAPACITY + place - base
            )
            spot = jnp.where(used, spot, 0)
            inner = pl.multiple_of(a_slot % held * ROWS, ROWS)
            left = a_v[a_slot // held, pl.ds(inner, ROWS), :]
            block = b_v[pl.ds(pl.multiple_of(spot * ROWS, ROWS), ROWS), :]
            turned = jnp.concatenate([block[:, BS:], block[:, :BS]], axis=1)
            right = jnp.concatenate(
                [
                    jnp.where(low, block, nothing),
                    jnp.where(low, turned, nothing),
                    jnp.where(low, nothing, turned),
                    jnp.where(low, nothing, block),
                ],
                axis=0,
            )
            term = jnp.dot(left, right, preferred_element_type=F32)
            i = jnp.where(used, target // kept, row_count)
            m = target % kept
            sums[i, pl.ds(m, ROWS, stride=kept), :] += term
        return carry

    lax.fori_loop(0, (total[0] + UNROLL - 1) // UNROLL, some_items, 0)

    def one_row(i, carry):
        for t in range(ROWS):
            piece = sums[i, pl.ds(t * kept, kept), :]
            if previous is not None:
                piece = piece + previous[i, :, pl.ds(t * LANES, LANES)]
            out[i, :, pl.ds(t * LANES, LANES)] = piece
        return carry

    lax.fori_loop(0, row_count, one_row, 0)


def multiply(base, previous, items, total, most, a_parts, own, b_parts, shape):
    first = base is None
    cols, peers = len(a_parts), len(b_parts) + 1
    any_spec = pl.BlockSpec(memory_space=pl.ANY)
    smem_spec = pl.BlockSpec(memory_space=SMEM)
    vmem_spec = pl.BlockSpec(memory_space=VMEM)
    given = [] if first else [base, previous]
    specs = [] if first else [smem_spec, vmem_spec]
    stored = own.shape[0] + (peers - 1) * CAPACITY * ROWS
    return pl.pallas_call(
        functools.partial(multiply_kernel, first, peers, cols),
        out_shape=[jax.ShapeDtypeStruct(shape, F32), jax.ShapeDtypeStruct((1,), I32)],
        in_specs=specs + [smem_spec] * 2 + [vmem_spec] + [any_spec] * (cols + peers),
        out_specs=[vmem_spec, smem_spec],
        scratch_shapes=[
            VMEM((cols,) + a_parts[0].shape, BF16),
            VMEM((stored, LANES), BF16),
            VMEM(((peers - 1) * FLAG, LANES), BF16),
            VMEM((shape[0] + 1, ROWS * shape[1], LANES), F32),
            pltpu.SemaphoreType.DMA((cols + 2 * peers - 1,)),
        ],
        compiler_params=pltpu.CompilerParams(vmem_limit_bytes=32 << 20),
        cost_estimate=pl.CostEstimate(flops=1 << 26, bytes_accessed=4 << 20, transcendentals=0),
        name="multiply",
    )(*given, items, total, most, *a_parts, own, *b_parts)


def send_rows(parts):
    return [shifted(part, "row", -(d + 1)) for d, part in enumerate(parts)]


def shards(a_blocks, a_index, b_blocks, b_cols, c_cols):
    rows = lax.axis_size("row")
    cols = lax.axis_size("col")
    per_col = rows // cols
    a_slots = a_blocks.shape[1] // per_col
    row_count = b_blocks.shape[0]
    span = -(-rows * row_count // cols // WORD) * WORD
    told = describe(a_index, b_cols.T, c_cols.T)
    told_all = lax.all_gather(told, ("row", "col"))
    packed, most = pack(None, told_all, b_blocks, rows, per_col, a_slots)
    arrived = send_rows(packed)
    a_late, b_late, _ = lax.optimization_barrier((a_blocks, b_blocks, most))
    a_ready, own = layout(a_late, b_late)
    a_parts = [a_ready] + [shifted(a_ready, "col", -h) for h in range(1, cols)]
    items, total = work_list(told_all, rows, row_count, span, per_col, a_slots)
    shape = (row_count, c_cols.shape[1], BS * BS)
    sums, rounds = multiply(None, None, items, total, most, a_parts, own, arrived, shape)

    def more(state):
        return state[0] < rounds[0]

    def one_round(state):
        at, sums = state
        base = jnp.reshape(at * CAPACITY, (1,))
        packed, _ = pack(base, told_all, b_blocks, rows, per_col, a_slots)
        arrived = send_rows(packed)
        sums, _ = multiply(base, sums, items, total, most, a_parts, own, arrived, shape)
        return at + 1, sums

    return lax.while_loop(more, one_round, (jnp.int32(1), sums))[1]


def solution(mesh):
    return jax.shard_map(
        shards,
        mesh=mesh,
        in_specs=(
            P(("sys", "row"), "col", None),
            P(None, ("sys", "row"), "col"),
            P(("sys", "row"), "col", None),
            P(("sys", "row"), "col"),
            P(("sys", "row"), "col"),
        ),
        out_specs=P(("sys", "row"), "col", None),
        check_vma=False,
    )
```

time: 46.4 us -> 48 us (1.034)
  starting transfers between devices: 17.2 us -> 2.43 us
  blocking collectives: 9.07 us -> 23.5 us
  waiting for transfers between devices: 0.03 us -> 4.58 us
  local copies, waits for them, and re-layouts: 2.91 us -> 0.97 us
  Pallas kernels: 16.3 us -> 15.7 us
    all_gather x1, blocking collectives: 9.07 us -> 23.5 us  [shards(): told_all = lax.all_gather(told, ('row', 'col'))]
    ppermute x6, starting transfers between devices: 10.8 us -> 2.43 us  [shifted(): return lax.ppermute(block, axis, route)]
    ppermute x4 -> x0, starting transfers between devices: 6.33 us -> none  [index_parts(): parts.append(lax.ppermute(told, ('row', 'col'), route))]
    ppermute x6, waiting for transfers between devices: 0.02 us -> 4.58 us  [shifted(): return lax.ppermute(block, axis, route)]
    unnamed x6, local copies, waits for them, and re-layouts: 2.91 us -> 0.97 us
    pallas_call x5, Pallas kernels: 16.3 us -> 15.7 us  [the longest x1 5.81 us: work_list(): pl.pallas_call(functools.partial(list_kernel, span, per_col, a_slots, pee...]
  transfers between devices with their start and end apart: 10 -> 6, of which waited for: 0 -> 2; matrix products, arithmetic and copies ran while one was open for 0% -> 0% of each run, Pallas kernels for 16% -> 12%
where the time goes in v3:
time: 48 us; the launch traced here: 47.9 us
  blocking collectives  23.5 us (49%)
  Pallas kernels  15.7 us (33%)
  waiting for transfers between devices  4.58 us (10%)
  starting transfers between devices  2.43 us (5%)
  local copies, waits for them, and re-layouts  0.97 us (2%)
  loops' own time  0.7 us (1%)
    all_gather x1, blocking collectives, shards(): told_all = lax.all_gather(told, ('row', 'col'))  23.5 us
    pallas_call x1, Pallas kernels, work_list(): pl.pallas_call(functools.partial(list_kernel, span, per_col, a_slots, pee...  5.81 us
    pallas_call x1, Pallas kernels, multiply(): pl.pallas_call(functools.partial(multiply_kernel, first, peers, cols), ou...  4.59 us
    ppermute x6, waiting for transfers between devices, shifted(): return lax.ppermute(block, axis, route)  4.58 us
    pallas_call x1, Pallas kernels, pack(): pl.pallas_call(functools.partial(pack_kernel, first, peers, per_col, a_sl...  3.09 us
    ppermute x6, starting transfers between devices, shifted(): return lax.ppermute(block, axis, route)  2.43 us
    pallas_call x1, Pallas kernels, describe(): pl.pallas_call(describe_kernel, out_shape=jax.ShapeDtypeStruct((TOLD, LAN...  1.44 us
    unnamed x6, local copies, waits for them, and re-layouts  0.97 us
  transfers between devices with their start and end apart: 6, of which 2 were waited for; matrix products, arithmetic and copies ran while one was open for 0% of the time, Pallas kernels for 12%

profile of v3, /device:TPU:0, one launch (start us, length us, event | category | flops | bytes accessed | tf_op | source)
XLA Modules:
  0.0 47.9 jit_solution(9021088574426025208)
XLA Ops:
  0.0 0.0 copy-start.2
  0.0 1.4 %describe.1 = s32[8,128]{1,0:T(8,128)} custom-call(s32[2,1,16]{2,1,0:T(1,128)} %a_ref.1, s32[4,16]{1,0:T(4,128)} %bitcast.11, s32[4,16]{1,0:T(4,128)} %bitcast.12), custom_call_target="tpu_custom_call" | custom-call | tf_op jit(solution)/shard_map/describe/pallas_call | solution.py:48
  1.4 23.5 %all-gather = s32[128,128]{1,0:T(8,128)S(1)} all-gather(s32[8,128]{1,0:T(8,128)} %describe.1), channel_id=2, replica_groups=mesh['sys'=2,'row'=4,'col'=4] {'row','col'}, dimensions={0}, use_global_device_ids=true | all-gather | bytes 69632 | tf_op jit(solution)/shard_map/all_gather | solution.py:435
  24.9 0.0 copy-start
  24.9 3.1 %pack.2 = (bf16[528,128]{1,0:T(8,128)(2,1)S(1)}, bf16[528,128]{1,0:T(8,128)(2,1)S(1)}, bf16[528,128]{1,0:T(8,128)(2,1)S(1)}, f32[8,128]{1,0:T(8,128)S(1)}) custom-call(s32[16,8,128]{2,1,0:T(8,128)S(1)} %bitcast.8, bf16[16,4,4096]{2,1,0:T(4,128)(2,1)} %b_ref), custom_call_target="tpu_custom_call" | custom-call | flops 1048576 | bytes 4194304 | tf_op jit(solution)/shard_map/pack/pallas_call | solution.py:192
  28.0 0.0 copy-done.2
  28.0 0.0 copy-done
  28.0 0.8 %layout.1 = (bf16[512,128]{1,0:T(8,128)(2,1)S(1)}, bf16[2048,128]{1,0:T(8,128)(2,1)S(1)}) custom-call(bf16[1,16,4096]{2,1,0:T(8,128)(2,1)S(1)} %copy-done, bf16[16,4,4096]{2,1,0:T(4,128)(2,1)S(1)} %copy-done.2), custom_call_target="tpu_custom_call" | custom-call | flops 16777216 | bytes 4194304 | tf_op jit(solution)/shard_map/layout/pallas_call | solution.py:109
  28.8 0.4 collective-permute-start.5
  29.2 0.0 collective-permute-start.6
  29.2 0.2 collective-permute-start.7
  29.4 1.8 %collective-permute-start.8 = (bf16[528,128]{1,0:T(8,128)(2,1)S(1)}, bf16[528,128]{1,0:T(8,128)(2,1)S(1)}, u32[]{:S(2)}, u32[]{:S(2)}) collective-permute-start(bf16[528,128]{1,0:T(8,128)(2,1)S(1)} %get-tuple-element.98), channel_id=1, source_target_pairs={{0,4},{4,8},{8,12},{12,0},{1,5},{5,9},{9,13},{13,1},{2,6},{6,10},{... | collective-permute-start | bytes 405512 | tf_op jit(solution)/shard_map/ppermute | solution.py:29
  31.2 0.0 collective-permute-start.4
  31.2 2.0 %collective-permute-done.5.refs_6_ = bf16[512,128]{1,0:T(8,128)(2,1)S(1)} collective-permute-done((bf16[512,128]{1,0:T(8,128)(2,1)S(1)}, bf16[512,128]{1,0:T(8,128)(2,1)S(1)}, u32[]{:S(2)}, u32[]{:S(2)}) %collective-permute-start.5) | collective-permute-done | bytes 131104 | tf_op jit(solution)/shard_map/ppermute | solution.py:29
  33.2 0.0 collective-permute-start.3
  33.2 5.8 %work_list.1 = (s32[264]{0:T(512)S(1)}, s32[1]{0:T(128)}) custom-call(s32[16,8,128]{2,1,0:T(8,128)S(1)} %bitcast.9), custom_call_target="tpu_custom_call" | custom-call | flops 1048576 | bytes 65536 | tf_op jit(solution)/shard_map/work_list/pallas_call | solution.py:290
  39.0 0.0 collective-permute-done.4.refs_5_
  39.1 0.0 collective-permute-done.3.refs_4_
  39.1 0.0 collective-permute-done.6.refs_8_
  39.1 2.5 %collective-permute-done.7.refs_9_ = bf16[528,128]{1,0:T(8,128)(2,1)S(1)} collective-permute-done((bf16[528,128]{1,0:T(8,128)(2,1)S(1)}, bf16[528,128]{1,0:T(8,128)(2,1)S(1)}, u32[]{:S(2)}, u32[]{:S(2)}) %collective-permute-start.7) | collective-permute-done | bytes 135200 | tf_op jit(solution)/shard_map/ppermute | solution.py:29
  41.6 0.0 collective-permute-done.8.refs_10_
  41.6 4.6 %multiply.2 = (f32[16,4,4096]{2,1,0:T(4,128)S(1)}, s32[1]{0:T(128)}) custom-call(s32[264]{0:T(512)S(1)} %get-tuple-element.221.refs_0_, s32[1]{0:T(128)} %get-tuple-element.222.refs_1_, f32[8,128]{1,0:T(8,128)S(1)} %get-tuple-element.223.refs_2_, bf16[512,128]{1,0:T(8,128)(2,1)S(1)} %get-tuple-element.224.refs_3_, ...), custom_call_target="tpu_custom_call" | custom-call | flops 67108864 | bytes 4194304 | tf_op jit(solution)/shard_map/multiply/pallas_call | solution.py:405
  46.2 0.7 %while.10 = (s32[]{:T(128)}, f32[16,4,4096]{2,1,0:T(4,128)S(1)}, s32[1]{0:T(128)}, s32[16,8,128]{2,1,0:T(8,128)S(1)}, bf16[16,4,4096]{2,1,0:T(4,128)(2,1)S(1)}, ...) while((s32[]{:T(128)}, f32[16,4,4096]{2,1,0:T(4,128)S(1)}, ...), condition=%wide.region_1.0_spmd, body=%wide.region_0.0_spmd.sunk | while | flops 68157440 | bytes 12108049 | solution.py:456
  46.9 0.0 copy-start.1
  46.9 1.0 %copy-done.1 = f32[16,4,4096]{2,1,0:T(4,128)} copy-done((f32[16,4,4096]{2,1,0:T(4,128)}, f32[16,4,4096]{2,1,0:T(4,128)S(1)}, u32[]{:S(2)}) %copy-start.1) | copy-done | bytes 1048600
Async XLA Ops:
  0.0 28.0 %copy-start.2 = (bf16[16,4,4096]{2,1,0:T(4,128)(2,1)S(1)}, bf16[16,4,4096]{2,1,0:T(4,128)(2,1)}, u32[]{:S(2)}) copy-start(bf16[16,4,4096]{2,1,0:T(4,128)(2,1)} %b_ref) | copy-start | bytes 1572868
  24.9 3.1 %copy-start = (bf16[1,16,4096]{2,1,0:T(8,128)(2,1)S(1)}, bf16[1,16,4096]{2,1,0:T(8,128)(2,1)}, u32[]{:S(2)}) copy-start(bf16[1,16,4096]{2,1,0:T(8,128)(2,1)} %a_ref.2) | copy-start | bytes 393220
  28.8 4.4 %collective-permute-start.5 = (bf16[512,128]{1,0:T(8,128)(2,1)S(1)}, bf16[512,128]{1,0:T(8,128)(2,1)S(1)}, u32[]{:S(2)}, u32[]{:S(2)}) collective-permute-start(bf16[512,128]{1,0:T(8,128)(2,1)S(1)} %get-tuple-element.224.refs_3_), channel_id=1, source_target_pairs={{0,1},{1,2},{2,3},{3,0},{4,5},{5,6},{6,7},{7,4},{8,9},{9,10},{10,1... | collective-permute-start | bytes 393224 | tf_op jit(solution)/shard_map/ppermute | solution.py:29
  29.2 9.9 %collective-permute-start.6 = (bf16[528,128]{1,0:T(8,128)(2,1)S(1)}, bf16[528,128]{1,0:T(8,128)(2,1)S(1)}, u32[]{:S(2)}, u32[]{:S(2)}) collective-permute-start(bf16[528,128]{1,0:T(8,128)(2,1)S(1)} %get-tuple-element.96), channel_id=1, source_target_pairs={{0,12},{4,0},{8,4},{12,8},{1,13},{5,1},{9,5},{13,9},{2,14},{6,2},{... | collective-permute-start | bytes 405512 | tf_op jit(solution)/shard_map/ppermute | solution.py:29
  29.2 12.4 %collective-permute-start.7 = (bf16[528,128]{1,0:T(8,128)(2,1)S(1)}, bf16[528,128]{1,0:T(8,128)(2,1)S(1)}, u32[]{:S(2)}, u32[]{:S(2)}) collective-permute-start(bf16[528,128]{1,0:T(8,128)(2,1)S(1)} %get-tuple-element.97), channel_id=1, source_target_pairs={{0,8},{4,12},{8,0},{12,4},{1,9},{5,13},{9,1},{13,5},{2,10},{6,14},... | collective-permute-start | bytes 405512 | tf_op jit(solution)/shard_map/ppermute | solution.py:29
  29.4 12.2 %collective-permute-start.8 = (bf16[528,128]{1,0:T(8,128)(2,1)S(1)}, bf16[528,128]{1,0:T(8,128)(2,1)S(1)}, u32[]{:S(2)}, u32[]{:S(2)}) collective-permute-start(bf16[528,128]{1,0:T(8,128)(2,1)S(1)} %get-tuple-element.98), channel_id=1, source_target_pairs={{0,4},{4,8},{8,12},{12,0},{1,5},{5,9},{9,13},{13,1},{2,6},{6,10},{... | collective-permute-start | bytes 405512 | tf_op jit(solution)/shard_map/ppermute | solution.py:29
  31.2 7.8 %collective-permute-start.4 = (bf16[512,128]{1,0:T(8,128)(2,1)S(1)}, bf16[512,128]{1,0:T(8,128)(2,1)S(1)}, u32[]{:S(2)}, u32[]{:S(2)}) collective-permute-start(bf16[512,128]{1,0:T(8,128)(2,1)S(1)} %get-tuple-element.224.refs_3_), channel_id=1, source_target_pairs={{0,2},{1,3},{2,0},{3,1},{4,6},{5,7},{6,4},{7,5},{8,10},{9,11},{10,... | collective-permute-start | bytes 393224 | tf_op jit(solution)/shard_map/ppermute | solution.py:29
  33.2 5.8 %collective-permute-start.3 = (bf16[512,128]{1,0:T(8,128)(2,1)S(1)}, bf16[512,128]{1,0:T(8,128)(2,1)S(1)}, u32[]{:S(2)}, u32[]{:S(2)}) collective-permute-start(bf16[512,128]{1,0:T(8,128)(2,1)S(1)} %get-tuple-element.224.refs_3_), channel_id=1, source_target_pairs={{0,3},{1,0},{2,1},{3,2},{4,7},{5,4},{6,5},{7,6},{8,11},{9,8},{10,9... | collective-permute-start | bytes 393224 | tf_op jit(solution)/shard_map/ppermute | solution.py:29
  46.9 1.0 %copy-start.1 = (f32[16,4,4096]{2,1,0:T(4,128)}, f32[16,4,4096]{2,1,0:T(4,128)S(1)}, u32[]{:S(2)}) copy-start(f32[16,4,4096]{2,1,0:T(4,128)S(1)} %get-tuple-element.273) | copy-start | bytes 3145732
